TPU v7x, 128 devices: a whole 4x4x4 slice. The times are simulated.
128 devices in a mesh: prefix: 16 (over x_lo, y, core), blk: 8 (over x_hi, z).
Axes of the slice: x: 4 (x_hi: 2, x_lo: 2; x = x_hi * 2 + x_lo), y: 4, z: 4, core: 2. Of those that a mesh axis runs over, the one named last changes fastest.
Arguments:
- queries: bfloat16 [2048, 8192], P(('prefix', 'blk')), may hold values from -24 to 24
- row_prompt: int32 [2048], P(('prefix', 'blk')), may hold values from 0 to 15, as said below
- suffix_length: int32 [2048], P(('prefix', 'blk')), may hold values from 1 to 128, as said below
- result_slot: int32 [2048], P(('prefix', 'blk')), may hold values from 0 to 15, as said below
- prompt_keys: bfloat16 [16, 16384, 1024], P('prefix', 'blk'), may hold values from -3 to 3
- prompt_values: bfloat16 [16, 16384, 1024], P('prefix', 'blk'), may hold values from -6 to 6
- continuation_keys: bfloat16 [2048, 128, 1024], P(('prefix', 'blk')), may hold values from -12 to 12
- continuation_values: bfloat16 [2048, 128, 1024], P(('prefix', 'blk')), may hold values from -6 to 6
Outputs:
- output: bfloat16 [2048, 8192], P(('prefix', 'blk'))
Inputs may be any that keep to these rules, and one draw needn't show every extreme that they name: `row_prompt`: within the rows of one device, at most 2 rows name the same prompt; for every index of blk, one prompt is named by exactly 2 rows of every device with that index. `suffix_length`: every device holds a row of length 128. `result_slot`: within the 16 rows of one device the values are a permutation of 0 to 15.
All inputs are finite; a program needn't handle non-finite values.
Results may differ from a plain program's by a relative error of at most 0.005.
Values may be sent and summed in bfloat16 or wider, within the bound.
No kernel may reach another device: no remote copies, remote signals or barrier semaphores. Data moves between devices by JAX's collectives and lax.ppermute only.
A program may use at most 128 MiB of HBM per device.

v0:
```python
import jax
import jax.numpy as jnp
from jax import lax
from jax.sharding import PartitionSpec as P

QUERY_HEADS = 64
KEY_HEADS = 8
HEAD_WIDTH = 128
HEADS_PER_KEY = 8
CAP = 2


def passed_along(x, axis, by):
    peers = lax.axis_size(axis)
    return lax.ppermute(x, axis, [(i, (i + by) % peers) for i in range(peers)])


def settle(scores, visible):
    scores = scores * HEAD_WIDTH ** (-0.5)
    if visible is not None:
        scores = jnp.where(visible, scores, -jnp.inf)
    highest = jnp.max(scores, axis=-1)
    weights = jnp.exp(scores - highest[..., None])
    if visible is not None:
        weights = jnp.where(visible, weights, 0.0)
    weights = weights.astype(jnp.bfloat16)
    weight_sum = jnp.sum(weights.astype(jnp.float32), axis=-1)
    return (highest, weight_sum, weights)


def prefix_block(query_group_block, key_entries, value_entries):
    quantity = query_group_block.shape[0]
    per_head = query_group_block.reshape(quantity, KEY_HEADS, HEADS_PER_KEY, HEAD_WIDTH)
    scores = jnp.einsum("nkgd,tkd->nkgt", per_head, key_entries, preferred_element_type=jnp.float32)
    highest, weight_sum, weights = settle(scores, None)
    blended = jnp.einsum(
        "nkgt,tkd->nkgd", weights, value_entries, preferred_element_type=jnp.float32
    )
    means = (blended / weight_sum[..., None]).astype(jnp.bfloat16)
    return (
        means.reshape(quantity, QUERY_HEADS * HEAD_WIDTH),
        highest.reshape(quantity, QUERY_HEADS),
        weight_sum.reshape(quantity, QUERY_HEADS),
    )


def prefix_part(query_group_block, key_entries, value_entries):
    return prefix_block(query_group_block, key_entries, value_entries)


def suffix_part(queries, continuation_keys, continuation_values, suffix_length):
    count_of_rows = queries.shape[0]
    per_head = queries.reshape(count_of_rows, KEY_HEADS, HEADS_PER_KEY, HEAD_WIDTH)
    key_suffix_part = continuation_keys.reshape(count_of_rows, -1, KEY_HEADS, HEAD_WIDTH)
    value_suffix_part = continuation_values.reshape(count_of_rows, -1, KEY_HEADS, HEAD_WIDTH)
    scores = jnp.einsum(
        "nkgd,ntkd->nkgt", per_head, key_suffix_part, preferred_element_type=jnp.float32
    )
    visible = (jnp.arange(key_suffix_part.shape[1])[None, :] < suffix_length[:, None])[
        :, None, None, :
    ]
    highest, weight_sum, weights = settle(scores, visible)
    blended = jnp.einsum(
        "nkgt,ntkd->nkgd", weights, value_suffix_part, preferred_element_type=jnp.float32
    )
    return (
        blended.reshape(count_of_rows, QUERY_HEADS, HEAD_WIDTH),
        highest.reshape(count_of_rows, QUERY_HEADS),
        weight_sum.reshape(count_of_rows, QUERY_HEADS),
    )


def deposit(collected, fresh, offset):
    return tuple(
        (
            lax.dynamic_update_slice_in_dim(whole, piece_new, offset, 0)
            for whole, piece_new in zip(collected, fresh)
        )
    )


def combine(highs, weight_sums, means, along):
    overall = jnp.max(highs, axis=along, keepdims=True)
    scaled = jnp.exp(highs - overall) * weight_sums
    merged_sum = jnp.sum(scaled, axis=along)
    merged_blend = jnp.sum(scaled[..., None] * means, axis=along)
    return (jnp.squeeze(overall, along), merged_sum, merged_blend)


def local(
    queries,
    row_prompt,
    suffix_length,
    result_slot,
    prompt_keys,
    prompt_values,
    continuation_keys,
    continuation_values,
):
    groups = lax.axis_size("prefix")
    members = lax.axis_size("blk")
    count_of_rows = queries.shape[0]
    width = queries.shape[1]
    slot_count = groups * CAP
    indices = jnp.arange(count_of_rows)
    earlier = (row_prompt[:, None] == row_prompt[None, :]) & (indices[None, :] < indices[:, None])
    arrival = jnp.sum(earlier.astype(jnp.int32), axis=1)
    token_position = row_prompt * CAP + arrival
    chooser = jnp.arange(slot_count)[None, :] == token_position[:, None]
    outgoing = jnp.einsum(
        "rs,rw->sw", chooser.astype(jnp.bfloat16), queries, preferred_element_type=jnp.float32
    ).astype(jnp.bfloat16)
    arrived = lax.all_to_all(
        outgoing.reshape(groups, CAP, width), "prefix", split_axis=0, concat_axis=0, tiled=True
    )
    query_group_block = arrived.reshape(slot_count, width)
    key_entries = prompt_keys[0].reshape(-1, KEY_HEADS, HEAD_WIDTH)
    value_entries = prompt_values[0].reshape(-1, KEY_HEADS, HEAD_WIDTH)
    tail_blend, tail_high, tail_total = suffix_part(
        queries, continuation_keys, continuation_values, suffix_length
    )
    blank = (
        jnp.zeros((members * slot_count, width), jnp.bfloat16),
        jnp.zeros((members * slot_count, QUERY_HEADS), jnp.float32),
        jnp.zeros((members * slot_count, QUERY_HEADS), jnp.float32),
    )
    own_index = lax.axis_index("blk")
    started = deposit(
        blank, prefix_part(query_group_block, key_entries, value_entries), own_index * slot_count
    )

    def turn(turn_index, carried):
        current, collected = carried
        current = passed_along(current, "blk", 1)
        root = jnp.mod(own_index - turn_index, members)
        fresh = prefix_part(current, key_entries, value_entries)
        return (current, deposit(collected, fresh, root * slot_count))

    _, collected = lax.fori_loop(1, members, turn, (query_group_block, started))
    range_means, highest, totals = collected
    selector = chooser.astype(jnp.float32).reshape(count_of_rows, groups, CAP)

    def to_owner(tensor):
        tensor = tensor.reshape(members, groups, CAP, -1)
        return jnp.swapaxes(tensor, 0, 1).reshape(groups * members, CAP, -1)

    mean_parts = lax.all_to_all(
        to_owner(range_means), ("prefix", "blk"), split_axis=0, concat_axis=0, tiled=True
    )
    stat_parts = (
        lax.all_to_all(
            to_owner(highest), ("prefix", "blk"), split_axis=0, concat_axis=0, tiled=True
        ),
        lax.all_to_all(
            to_owner(totals), ("prefix", "blk"), split_axis=0, concat_axis=0, tiled=True
        ),
    )

    def select_rows(tensor):
        tensor = tensor.reshape(groups, members, CAP, -1)
        return jnp.einsum("rpc,pjcw->rjw", selector, tensor, precision=lax.Precision.HIGHEST)

    part_mean = select_rows(mean_parts.astype(jnp.float32)).reshape(
        count_of_rows, members, QUERY_HEADS, HEAD_WIDTH
    )
    part_high = select_rows(stat_parts[0])
    part_total = select_rows(stat_parts[1])
    pre_high, pre_total, pre_blend = combine(part_high, part_total, part_mean, 1)
    overall = jnp.maximum(pre_high, tail_high)
    leading = jnp.exp(pre_high - overall)
    trailing = jnp.exp(tail_high - overall)
    numerator = leading[..., None] * pre_blend + trailing[..., None] * tail_blend
    denominator = leading * pre_total + trailing * tail_total
    results = (numerator / denominator[..., None]).reshape(count_of_rows, width)
    placer = (indices[:, None] == result_slot[None, :]).astype(jnp.float32)
    return jnp.dot(placer, results, precision=lax.Precision.HIGHEST).astype(jnp.bfloat16)


def solution(mesh):
    in_specs = (
        P(("prefix", "blk"), None),
        P(("prefix", "blk")),
        P(("prefix", "blk")),
        P(("prefix", "blk")),
        P("prefix", "blk", None),
        P("prefix", "blk", None),
        P(("prefix", "blk"), None, None),
        P(("prefix", "blk"), None, None),
    )
    out_specs = P(("prefix", "blk"), None)
    return jax.shard_map(local, mesh=mesh, in_specs=in_specs, out_specs=out_specs, check_vma=False)
```

profile of v0, /device:TPU:1, one launch (start us, length us, event | category | flops | bytes accessed | tf_op | source)
XLA Modules:
  0.0 386.0 jit_solution(14295641416902914360)
XLA Ops:
  4.6 6.9 %all-to-all-start = ((bf16[16,2,8192]{2,1,0:T(2,128)(2,1)}), bf16[16,2,8192]{2,1,0:T(2,128)(2,1)S(1)}, u32[]{:S(2)}, u32[]{:S(2)}) async-start(bf16[16,2,8192]{2,1,0:T(2,128)(2,1)} %reshape.187), calls=%async_computation | async-start | bytes 1048576 | tf_op jit(solution)/shard_map/all_to_all | solution.py:113
  11.5 6.5 %copy.148 = bf16[1,2048,1024]{1,2,0:T(8,128)(2,1)} copy(bf16[1,2048,1024]{2,1,0:T(8,128)(2,1)} %param.14) | data formatting | bytes 8388608 | tf_op args[4]
  18.1 6.5 %copy.151 = bf16[1,2048,1024]{1,2,0:T(8,128)(2,1)} copy(bf16[1,2048,1024]{2,1,0:T(8,128)(2,1)} %param.15) | data formatting | bytes 8388608 | tf_op args[5]
  24.5 6.4 %copy.156 = bf16[2048,8,128]{2,0,1:T(8,128)(2,1)} copy(bf16[2048,8,128]{0,2,1:T(8,128)(2,1)} %bitcast.212) | data formatting | bytes 8388608 | tf_op jit(solution)/shard_map/while | solution.py:139
  31.0 6.5 %copy.157 = bf16[2048,8,128]{2,0,1:T(8,128)(2,1)} copy(bf16[2048,8,128]{0,2,1:T(8,128)(2,1)} %bitcast.214) | data formatting | bytes 8388608 | tf_op jit(solution)/shard_map/while | solution.py:139
  37.8 9.3 %bitcast_reduce_fusion.1 = (f32[32,8,8]{2,0,1:T(8,128)S(1)}, f32[8,32,8,2048]{3,2,1,0:T(8,128)}) fusion(bf16[2048,8,128,1]{0,2,3,1:T(8,128)(2,1)} %bitcast.213, bf16[32,8,8,128]{3,2,1,0:T(8,128)(2,1)S(1)} %reshape_reshape.3), kind=kOutput, calls=%fused_computation.15 | convolution fusion | flops 1082128384 | bytes 21504000 | tf_op jit(solution)/shard_map/nkgd,tkd->nkgt/dot_general | solution.py:34
  47.2 7.6 %convert_reduce_fusion.1 = f32[32,8,8]{2,0,1:T(8,128)S(1)} fusion(f32[32,8,8]{2,0,1:T(8,128)S(1)} %get-tuple-element.280, f32[8,32,8,2048]{3,2,1,0:T(8,128)} %get-tuple-element.281), kind=kLoop, calls=%fused_computation.18 | loop fusion | flops 20969472 | bytes 16793600 | tf_op jit(solution)/shard_map/reduce_sum | solution.py:27
  54.8 8.6 %divide_convert_fusion.1 = bf16[32,8,8,128]{3,2,0,1:T(8,128)(2,1)S(1)} fusion(bf16[2048,8,128,1]{0,2,3,1:T(8,128)(2,1)} %bitcast.215, f32[8,32,8,2048]{3,2,1,0:T(8,128)} %get-tuple-element.281, f32[32,8,8]{2,0,1:T(8,128)S(1)} %get-tuple-element.280, f32[32,8,8]{2,0,1:T(8,128)S(1)} %convert_reduce_fusion.1), kind=kOutput, calls=%fused_computation.40 | convolution fusion | flops 1086849024 | bytes 21512192 | tf_op jit(solution)/shard_map/nkgt,tkd->nkgd/dot_general | solution.py:36
  68.2 205.6 %while.21 = (s32[]{:T(128)}, bf16[32,8192]{1,0:T(8,128)(2,1)S(1)}, bf16[256,8192]{1,0:T(8,128)(2,1)}, f32[256,64]{0,1:T(8,128)S(1)}, f32[256,64]{0,1:T(8,128)S(1...) while((s32[]{:T(128)}, bf16[32,8192]{1,0:T(8,128)(2,1)S(1)}, ...), condition=%wide.region_6.7_spmd, body=%wide.region_3.6_spmd.sunk | while | flops 2189946880 | bytes 82911608 | solution.py:139
  70.5 16.2 %collective-permute-done = bf16[32,8192]{1,0:T(8,128)(2,1)S(1)} collective-permute-done((bf16[32,8192]{1,0:T(8,128)(2,1)S(1)}, bf16[32,8192]{1,0:T(8,128)(2,1)S(1)}, u32[]{:S(2)}, u32[]{:S(2)}) %collective-permute-start) | collective-permute-done | bytes 524320 | tf_op jit(solution)/shard_map/while/body/eval_jaxpr/ppermute | solution.py:15
  86.8 4.7 %bitcast_reduce_fusion.3 = (f32[32,8,8]{0,2,1:T(8,128)S(1)}, f32[8,2048,32,8]{1,2,3,0:T(8,128)S(1)}) fusion(bf16[32,8,8,128]{3,2,1,0:T(8,128)(2,1)S(1)} %bitcast.211, bf16[2048,8,128]{2,0,1:T(8,128)(2,1)} %get-tuple-element.372), kind=kOutput, calls=%fused_computation.1.clone.1 | convolution fusion | flops 1082128384 | bytes 21504000 | tf_op jit(solution)/shard_map/while/body/eval_jaxpr/nkgd,tkd->nkgt/dot_general | solution.py:34
  101.3 16.4 %collective-permute-done = bf16[32,8192]{1,0:T(8,128)(2,1)S(1)} collective-permute-done((bf16[32,8192]{1,0:T(8,128)(2,1)S(1)}, bf16[32,8192]{1,0:T(8,128)(2,1)S(1)}, u32[]{:S(2)}, u32[]{:S(2)}) %collective-permute-start) | collective-permute-done | bytes 524320 | tf_op jit(solution)/shard_map/while/body/eval_jaxpr/ppermute | solution.py:15
  117.8 4.7 %bitcast_reduce_fusion.3 = (f32[32,8,8]{0,2,1:T(8,128)S(1)}, f32[8,2048,32,8]{1,2,3,0:T(8,128)S(1)}) fusion(bf16[32,8,8,128]{3,2,1,0:T(8,128)(2,1)S(1)} %bitcast.211, bf16[2048,8,128]{2,0,1:T(8,128)(2,1)} %get-tuple-element.372), kind=kOutput, calls=%fused_computation.1.clone.1 | convolution fusion | flops 1082128384 | bytes 21504000 | tf_op jit(solution)/shard_map/while/body/eval_jaxpr/nkgd,tkd->nkgt/dot_general | solution.py:34
  132.3 15.4 %collective-permute-done = bf16[32,8192]{1,0:T(8,128)(2,1)S(1)} collective-permute-done((bf16[32,8192]{1,0:T(8,128)(2,1)S(1)}, bf16[32,8192]{1,0:T(8,128)(2,1)S(1)}, u32[]{:S(2)}, u32[]{:S(2)}) %collective-permute-start) | collective-permute-done | bytes 524320 | tf_op jit(solution)/shard_map/while/body/eval_jaxpr/ppermute | solution.py:15
  147.8 4.7 %bitcast_reduce_fusion.3 = (f32[32,8,8]{0,2,1:T(8,128)S(1)}, f32[8,2048,32,8]{1,2,3,0:T(8,128)S(1)}) fusion(bf16[32,8,8,128]{3,2,1,0:T(8,128)(2,1)S(1)} %bitcast.211, bf16[2048,8,128]{2,0,1:T(8,128)(2,1)} %get-tuple-element.372), kind=kOutput, calls=%fused_computation.1.clone.1 | convolution fusion | flops 1082128384 | bytes 21504000 | tf_op jit(solution)/shard_map/while/body/eval_jaxpr/nkgd,tkd->nkgt/dot_general | solution.py:34
  162.4 14.5 %collective-permute-done = bf16[32,8192]{1,0:T(8,128)(2,1)S(1)} collective-permute-done((bf16[32,8192]{1,0:T(8,128)(2,1)S(1)}, bf16[32,8192]{1,0:T(8,128)(2,1)S(1)}, u32[]{:S(2)}, u32[]{:S(2)}) %collective-permute-start) | collective-permute-done | bytes 524320 | tf_op jit(solution)/shard_map/while/body/eval_jaxpr/ppermute | solution.py:15
  177.0 4.7 %bitcast_reduce_fusion.3 = (f32[32,8,8]{0,2,1:T(8,128)S(1)}, f32[8,2048,32,8]{1,2,3,0:T(8,128)S(1)}) fusion(bf16[32,8,8,128]{3,2,1,0:T(8,128)(2,1)S(1)} %bitcast.211, bf16[2048,8,128]{2,0,1:T(8,128)(2,1)} %get-tuple-element.372), kind=kOutput, calls=%fused_computation.1.clone.1 | convolution fusion | flops 1082128384 | bytes 21504000 | tf_op jit(solution)/shard_map/while/body/eval_jaxpr/nkgd,tkd->nkgt/dot_general | solution.py:34
  191.2 13.6 %collective-permute-done = bf16[32,8192]{1,0:T(8,128)(2,1)S(1)} collective-permute-done((bf16[32,8192]{1,0:T(8,128)(2,1)S(1)}, bf16[32,8192]{1,0:T(8,128)(2,1)S(1)}, u32[]{:S(2)}, u32[]{:S(2)}) %collective-permute-start) | collective-permute-done | bytes 524320 | tf_op jit(solution)/shard_map/while/body/eval_jaxpr/ppermute | solution.py:15
  204.9 4.7 %bitcast_reduce_fusion.3 = (f32[32,8,8]{0,2,1:T(8,128)S(1)}, f32[8,2048,32,8]{1,2,3,0:T(8,128)S(1)}) fusion(bf16[32,8,8,128]{3,2,1,0:T(8,128)(2,1)S(1)} %bitcast.211, bf16[2048,8,128]{2,0,1:T(8,128)(2,1)} %get-tuple-element.372), kind=kOutput, calls=%fused_computation.1.clone.1 | convolution fusion | flops 1082128384 | bytes 21504000 | tf_op jit(solution)/shard_map/while/body/eval_jaxpr/nkgd,tkd->nkgt/dot_general | solution.py:34
  219.8 12.7 %collective-permute-done = bf16[32,8192]{1,0:T(8,128)(2,1)S(1)} collective-permute-done((bf16[32,8192]{1,0:T(8,128)(2,1)S(1)}, bf16[32,8192]{1,0:T(8,128)(2,1)S(1)}, u32[]{:S(2)}, u32[]{:S(2)}) %collective-permute-start) | collective-permute-done | bytes 524320 | tf_op jit(solution)/shard_map/while/body/eval_jaxpr/ppermute | solution.py:15
  232.5 4.7 %bitcast_reduce_fusion.3 = (f32[32,8,8]{0,2,1:T(8,128)S(1)}, f32[8,2048,32,8]{1,2,3,0:T(8,128)S(1)}) fusion(bf16[32,8,8,128]{3,2,1,0:T(8,128)(2,1)S(1)} %bitcast.211, bf16[2048,8,128]{2,0,1:T(8,128)(2,1)} %get-tuple-element.372), kind=kOutput, calls=%fused_computation.1.clone.1 | convolution fusion | flops 1082128384 | bytes 21504000 | tf_op jit(solution)/shard_map/while/body/eval_jaxpr/nkgd,tkd->nkgt/dot_general | solution.py:34
  247.4 11.6 %collective-permute-done = bf16[32,8192]{1,0:T(8,128)(2,1)S(1)} collective-permute-done((bf16[32,8192]{1,0:T(8,128)(2,1)S(1)}, bf16[32,8192]{1,0:T(8,128)(2,1)S(1)}, u32[]{:S(2)}, u32[]{:S(2)}) %collective-permute-start) | collective-permute-done | bytes 524320 | tf_op jit(solution)/shard_map/while/body/eval_jaxpr/ppermute | solution.py:15
  259.1 4.7 %bitcast_reduce_fusion.3 = (f32[32,8,8]{0,2,1:T(8,128)S(1)}, f32[8,2048,32,8]{1,2,3,0:T(8,128)S(1)}) fusion(bf16[32,8,8,128]{3,2,1,0:T(8,128)(2,1)S(1)} %bitcast.211, bf16[2048,8,128]{2,0,1:T(8,128)(2,1)} %get-tuple-element.372), kind=kOutput, calls=%fused_computation.1.clone.1 | convolution fusion | flops 1082128384 | bytes 21504000 | tf_op jit(solution)/shard_map/while/body/eval_jaxpr/nkgd,tkd->nkgt/dot_general | solution.py:34
  274.9 9.7 %all-to-all-start.1 = ((f32[128,1,128]{2,1,0:T(1,128)}), f32[128,1,128]{2,1,0:T(1,128)S(1)}, u32[]{:S(2)}, u32[]{:S(2)}) async-start(f32[128,1,128]{2,1,0:T(1,128)} %reshape.216), calls=%async_computation.1 | async-start | bytes 131072 | tf_op jit(solution)/shard_map/all_to_all | solution.py:151
  285.7 8.4 %all-to-all-done.1 = f32[128,1,128]{2,1,0:T(1,128)S(1)} async-done(((f32[128,1,128]{2,1,0:T(1,128)}), f32[128,1,128]{2,1,0:T(1,128)S(1)}, u32[]{:S(2)}, u32[]{:S(2)}) %all-to-all-start.1) | async-done | bytes 65568 | tf_op jit(solution)/shard_map/all_to_all | solution.py:151
  294.1 4.6 %all-to-all-start.2 = ((f32[128,1,128]{2,1,0:T(1,128)}), f32[128,1,128]{2,1,0:T(1,128)S(1)}, u32[]{:S(2)}, u32[]{:S(2)}) async-start(f32[128,1,128]{2,1,0:T(1,128)} %reshape.218), calls=%async_computation.2 | async-start | bytes 131072 | tf_op jit(solution)/shard_map/all_to_all | solution.py:154
  298.7 7.6 %reshape.201 = bf16[8,16,2,8192]{3,2,1,0:T(2,128)(2,1)} reshape(bf16[256,8192]{1,0:T(8,128)(2,1)} %get-tuple-element.208) | data formatting | bytes 8388608 | tf_op jit(solution)/shard_map/reshape | solution.py:144
  306.3 4.9 %copy.269 = bf16[16,8,2,8192]{3,1,0,2:T(8,128)(2,1)S(1)} copy(bf16[16,8,2,8192]{3,2,0,1:T(2,128)(2,1)} %bitcast.216) | data formatting | bytes 8388608 | tf_op jit(solution)/shard_map/transpose | solution.py:145
  311.2 6.3 %copy.174 = bf16[128,2,8192]{2,1,0:T(2,128)(2,1)} copy(bf16[128,2,8192]{2,0,1:T(8,128)(2,1)S(1)} %bitcast.217) | data formatting | bytes 8388608 | tf_op jit(solution)/shard_map/reshape | solution.py:145
  317.5 10.2 %all-to-all-start.3 = ((bf16[128,2,8192]{2,1,0:T(2,128)(2,1)}), bf16[128,2,8192]{2,1,0:T(2,128)(2,1)}, u32[]{:S(2)}, u32[]{:S(2)}) async-start(bf16[128,2,8192]{2,1,0:T(2,128)(2,1)} %copy.174), calls=%async_computation.3 | async-start | bytes 8388608 | tf_op jit(solution)/shard_map/all_to_all | solution.py:147
  339.9 38.0 %all-to-all-done.3 = bf16[128,2,8192]{2,1,0:T(2,128)(2,1)} async-done(((bf16[128,2,8192]{2,1,0:T(2,128)(2,1)}), bf16[128,2,8192]{2,1,0:T(2,128)(2,1)}, u32[]{:S(2)}, u32[]{:S(2)}) %all-to-all-start.3) | async-done | bytes 4194336 | tf_op jit(solution)/shard_map/all_to_all | solution.py:147
  377.9 5.5 %fusion.27 = f32[16,64,128]{2,0,1:T(8,128)S(1)} fusion(f32[16,8,64]{0,2,1:T(8,128)S(1)} %copy.172, s32[16,2]{0,1:T(2,128)S(1)} %multiply_add_fusion.1, s32[16]{0:T(128)S(1)} %copy-done.3, bf16[16,8,2,8192]{3,2,1,0:T(2,128)(2,1)} %bitcast.34), kind=kOutput, calls=%fused_computation.31 | convolution fusion | flops 69075456 | bytes 4751552 | tf_op jit(solution)/shard_map/rpc,pjcw->rjw/dot_general | solution.py:161
  (135 shorter events, 98.2 us)
Async XLA Ops:
  1.6 0.6 copy-start.2
  4.6 32.8 %all-to-all-start = ((bf16[16,2,8192]{2,1,0:T(2,128)(2,1)}), bf16[16,2,8192]{2,1,0:T(2,128)(2,1)S(1)}, u32[]{:S(2)}, u32[]{:S(2)}) async-start(bf16[16,2,8192]{2,1,0:T(2,128)(2,1)} %reshape.187), calls=%async_computation | async-start | bytes 1048576 | tf_op jit(solution)/shard_map/all_to_all | solution.py:113
  68.4 18.2 %collective-permute-start = (bf16[32,8192]{1,0:T(8,128)(2,1)S(1)}, bf16[32,8192]{1,0:T(8,128)(2,1)S(1)}, u32[]{:S(2)}, u32[]{:S(2)}) collective-permute-start(bf16[32,8192]{1,0:T(8,128)(2,1)S(1)} %get-tuple-element.354), channel_id=1, source_target_pairs={{0,1},{1,2},{2,3},{3,4},{4,5},{5,6},{6,7},{7,0},{8,9},{9,10},{10,1... | collective-permute-start | bytes 1572872 | tf_op jit(solution)/shard_map/while/body/eval_jaxpr/ppermute | solution.py:15
  91.4 3.4 copy-start
  101.2 16.5 %collective-permute-start = (bf16[32,8192]{1,0:T(8,128)(2,1)S(1)}, bf16[32,8192]{1,0:T(8,128)(2,1)S(1)}, u32[]{:S(2)}, u32[]{:S(2)}) collective-permute-start(bf16[32,8192]{1,0:T(8,128)(2,1)S(1)} %get-tuple-element.354), channel_id=1, source_target_pairs={{0,1},{1,2},{2,3},{3,4},{4,5},{5,6},{6,7},{7,0},{8,9},{9,10},{10,1... | collective-permute-start | bytes 1572872 | tf_op jit(solution)/shard_map/while/body/eval_jaxpr/ppermute | solution.py:15
  122.4 3.4 copy-start
  132.2 15.5 %collective-permute-start = (bf16[32,8192]{1,0:T(8,128)(2,1)S(1)}, bf16[32,8192]{1,0:T(8,128)(2,1)S(1)}, u32[]{:S(2)}, u32[]{:S(2)}) collective-permute-start(bf16[32,8192]{1,0:T(8,128)(2,1)S(1)} %get-tuple-element.354), channel_id=1, source_target_pairs={{0,1},{1,2},{2,3},{3,4},{4,5},{5,6},{6,7},{7,0},{8,9},{9,10},{10,1... | collective-permute-start | bytes 1572872 | tf_op jit(solution)/shard_map/while/body/eval_jaxpr/ppermute | solution.py:15
  152.5 3.4 copy-start
  162.3 14.6 %collective-permute-start = (bf16[32,8192]{1,0:T(8,128)(2,1)S(1)}, bf16[32,8192]{1,0:T(8,128)(2,1)S(1)}, u32[]{:S(2)}, u32[]{:S(2)}) collective-permute-start(bf16[32,8192]{1,0:T(8,128)(2,1)S(1)} %get-tuple-element.354), channel_id=1, source_target_pairs={{0,1},{1,2},{2,3},{3,4},{4,5},{5,6},{6,7},{7,0},{8,9},{9,10},{10,1... | collective-permute-start | bytes 1572872 | tf_op jit(solution)/shard_map/while/body/eval_jaxpr/ppermute | solution.py:15
  181.7 3.4 copy-start
  191.1 13.7 %collective-permute-start = (bf16[32,8192]{1,0:T(8,128)(2,1)S(1)}, bf16[32,8192]{1,0:T(8,128)(2,1)S(1)}, u32[]{:S(2)}, u32[]{:S(2)}) collective-permute-start(bf16[32,8192]{1,0:T(8,128)(2,1)S(1)} %get-tuple-element.354), channel_id=1, source_target_pairs={{0,1},{1,2},{2,3},{3,4},{4,5},{5,6},{6,7},{7,0},{8,9},{9,10},{10,1... | collective-permute-start | bytes 1572872 | tf_op jit(solution)/shard_map/while/body/eval_jaxpr/ppermute | solution.py:15
  209.6 3.4 copy-start
  219.7 12.8 %collective-permute-start = (bf16[32,8192]{1,0:T(8,128)(2,1)S(1)}, bf16[32,8192]{1,0:T(8,128)(2,1)S(1)}, u32[]{:S(2)}, u32[]{:S(2)}) collective-permute-start(bf16[32,8192]{1,0:T(8,128)(2,1)S(1)} %get-tuple-element.354), channel_id=1, source_target_pairs={{0,1},{1,2},{2,3},{3,4},{4,5},{5,6},{6,7},{7,0},{8,9},{9,10},{10,1... | collective-permute-start | bytes 1572872 | tf_op jit(solution)/shard_map/while/body/eval_jaxpr/ppermute | solution.py:15
  237.2 3.4 copy-start
  247.3 11.7 %collective-permute-start = (bf16[32,8192]{1,0:T(8,128)(2,1)S(1)}, bf16[32,8192]{1,0:T(8,128)(2,1)S(1)}, u32[]{:S(2)}, u32[]{:S(2)}) collective-permute-start(bf16[32,8192]{1,0:T(8,128)(2,1)S(1)} %get-tuple-element.354), channel_id=1, source_target_pairs={{0,1},{1,2},{2,3},{3,4},{4,5},{5,6},{6,7},{7,0},{8,9},{9,10},{10,1... | collective-permute-start | bytes 1572872 | tf_op jit(solution)/shard_map/while/body/eval_jaxpr/ppermute | solution.py:15
  263.8 3.4 copy-start
  274.9 19.2 %all-to-all-start.1 = ((f32[128,1,128]{2,1,0:T(1,128)}), f32[128,1,128]{2,1,0:T(1,128)S(1)}, u32[]{:S(2)}, u32[]{:S(2)}) async-start(f32[128,1,128]{2,1,0:T(1,128)} %reshape.216), calls=%async_computation.1 | async-start | bytes 131072 | tf_op jit(solution)/shard_map/all_to_all | solution.py:151
  294.1 23.5 %all-to-all-start.2 = ((f32[128,1,128]{2,1,0:T(1,128)}), f32[128,1,128]{2,1,0:T(1,128)S(1)}, u32[]{:S(2)}, u32[]{:S(2)}) async-start(f32[128,1,128]{2,1,0:T(1,128)} %reshape.218), calls=%async_computation.2 | async-start | bytes 131072 | tf_op jit(solution)/shard_map/all_to_all | solution.py:154
  317.5 10.3 %copy-start.1 = (bf16[16,8192]{1,0:T(8,128)(2,1)S(1)}, bf16[16,8192]{1,0:T(8,128)(2,1)}, u32[]{:S(2)}) copy-start(bf16[16,8192]{1,0:T(8,128)(2,1)} %param.10) | copy-start | bytes 786436
  317.5 10.3 %copy-start.4 = (s32[16]{0:T(128)S(1)}, s32[16]{0:T(128)}, u32[]{:S(2)}) copy-start(s32[16]{0:T(128)} %param.12) | copy-start | bytes 196
  317.5 60.4 %all-to-all-start.3 = ((bf16[128,2,8192]{2,1,0:T(2,128)(2,1)}), bf16[128,2,8192]{2,1,0:T(2,128)(2,1)}, u32[]{:S(2)}, u32[]{:S(2)}) async-start(bf16[128,2,8192]{2,1,0:T(2,128)(2,1)} %copy.174), calls=%async_computation.3 | async-start | bytes 8388608 | tf_op jit(solution)/shard_map/all_to_all | solution.py:147
  332.4 6.6 %copy-start.3 = (s32[16]{0:T(128)S(1)}, s32[16]{0:T(128)}, u32[]{:S(2)}) copy-start(s32[16]{0:T(128)} %copy-done.2) | copy-start | bytes 196
  377.9 5.9 %copy-start.5 = (s32[16]{0:T(128)S(1)}, s32[16]{0:T(128)}, u32[]{:S(2)}) copy-start(s32[16]{0:T(128)} %param.13) | copy-start | bytes 196
where the time goes:
time: 388 us; the launch traced here: 386 us
  waiting for transfers between devices  147 us (38%)
  matrix products  97 us (25%)
  local copies, waits for them, and re-layouts  72.3 us (19%)
  other arithmetic  34.8 us (9%)
  starting transfers between devices  34 us (9%)
    ppermute x7, waiting for transfers between devices, passed_along(): return lax.ppermute(x, axis, [(i, (i + by) % peers) for i in range(peers)])  100 us
    dot_general x8, matrix products, prefix_block(): jnp.einsum('nkgd,tkd->nkgt', per_head, key_entries, preferred_element_typ...  42 us
    all_to_all x1, waiting for transfers between devices, local(): lax.all_to_all(to_owner(range_means), ('prefix', 'blk'), split_axis=0, co...  38 us
    dot_general x8, matrix products, prefix_block(): jnp.einsum('nkgt,tkd->nkgd', weights, value_entries, preferred_element_ty...  37.5 us
    reduce_sum x9, other arithmetic, settle(): weight_sum = jnp.sum(weights.astype(jnp.float32), axis=-1)  31.5 us
    dynamic_update_slice x24, local copies, waits for them, and re-layouts, deposit(): lax.dynamic_update_slice_in_dim(whole, piece_new, offset, 0)  16.2 us
    unnamed x17, local copies, waits for them, and re-layouts  15.4 us
    while x4, local copies, waits for them, and re-layouts, local(): _, collected = lax.fori_loop(1, members, turn, (query_group_block, started))  13.1 us
  transfers between devices with their start and end apart: 11, of which 9 were waited for; matrix products, arithmetic and copies ran while one was open for 15% of the time, Pallas kernels for 0%

commit v1 on v0

v1 whole, which is shorter than its diff:
```python
import functools

import jax
import jax.numpy as jnp
from jax import lax
from jax.experimental import pallas as pl
from jax.experimental.pallas import tpu as pltpu
from jax.sharding import Mesh
from jax.sharding import PartitionSpec as P

KEY_HEADS = 8
HEAD_WIDTH = 128
HEADS_PER_KEY = 8
KEY_SPAN = HEADS_PER_KEY * HEAD_WIDTH
CAP = 2
Z = 4
GROUPS = 2
STAT = 32
SCALE = HEAD_WIDTH ** (-0.5) * 1.4426950408889634
MIB = 1024 * 1024
F32 = jnp.float32
BF16 = jnp.bfloat16


def params(mib):
    return pltpu.CompilerParams(vmem_limit_bytes=mib * MIB)


def lanes(shape):
    return lax.broadcasted_iota(jnp.int32, shape, len(shape) - 1)


def encode(stat):
    hi = stat.astype(BF16)
    rest = stat - hi.astype(F32)
    mid = rest.astype(BF16)
    lo = (rest - mid.astype(F32)).astype(BF16)
    lane = lanes(stat.shape)
    return jnp.where(
        lane < STAT, hi.astype(F32), jnp.where(lane < 2 * STAT, mid.astype(F32), lo.astype(F32))
    ).astype(BF16)


def decode(plane):
    plane = plane.astype(F32)
    return plane + pltpu.roll(plane, 128 - STAT, 1) + pltpu.roll(plane, 128 - 2 * STAT, 1)


def prefix_kernel(rows, many, *refs):
    q_refs, (k_ref, v_ref) = refs[:many], refs[many : many + 2]
    out_refs, wide, stat = refs[-2 - many : -2], refs[-2], refs[-1]
    step = pl.program_id(0)
    width = out_refs[0].shape[1] - 128

    @pl.when(step == 0)
    def _():
        wide[:, HEAD_WIDTH:] = jnp.ones((wide.shape[0], HEAD_WIDTH), BF16)
        stat[...] = jnp.zeros_like(stat)

    wide[:, :HEAD_WIDTH] = v_ref[...]
    per_tile = 256 // rows
    lane = lanes((rows, 128))
    tiles = [(i, h) for i in range(many) for h in range(0, HEADS_PER_KEY, per_tile)]
    gathered = [stat[i] for i in range(many)]

    def columns(h):
        return pl.ds(pl.multiple_of(step * KEY_SPAN + h * HEAD_WIDTH, HEAD_WIDTH), HEAD_WIDTH)

    def score(i, first):
        q = jnp.concatenate([q_refs[i][:, columns(first + j)] for j in range(per_tile)], axis=0)
        return lax.dot_general(
            q, k_ref[...], (((1,), (1,)), ((), ())), preferred_element_type=F32
        )

    scores = score(*tiles[0])
    waiting = None
    for n in range(len(tiles) + 1):
        ahead = score(*tiles[n + 1]) if n + 1 < len(tiles) else None
        if waiting is not None:
            both = jnp.dot(waiting[1], wide[...], preferred_element_type=F32)
        old = waiting
        if n < len(tiles):
            top = jnp.max(scores, axis=1, keepdims=True)
            waiting = (top, jnp.exp2((scores - top) * SCALE).astype(BF16))
        if old is not None:
            i, first = tiles[n - 1]
            total = both[:, HEAD_WIDTH:]
            mean = (both[:, :HEAD_WIDTH] / total).astype(BF16)
            level = old[0] * SCALE + jnp.log2(total)
            for j in range(per_tile):
                part = slice(j * rows, (j + 1) * rows)
                out_refs[i][:, columns(first + j)] = mean[part]
                here = lane % STAT == step * HEADS_PER_KEY + first + j
                gathered[i] = jnp.where(here, level[part], gathered[i])
        scores = ahead
    for i in range(many):
        stat[i] = gathered[i]

    @pl.when(step == pl.num_programs(0) - 1)
    def _():
        for i in range(many):
            out_refs[i][:, width:] = encode(gathered[i])


def prefix_part(queries, keys, values, group, after=()):
    many = len(queries)
    rows, width = queries[0].shape
    count = width // KEY_SPAN
    length = keys.shape[0]
    entry = pl.BlockSpec((length, HEAD_WIDTH), lambda k: (0, group * count + k))
    block = pl.BlockSpec((rows, width), lambda k: (0, 0))
    return pl.pallas_call(
        functools.partial(prefix_kernel, rows, many),
        grid=(count,),
        in_specs=[block] * many
        + [entry, entry]
        + [pl.BlockSpec(memory_space=pl.ANY)] * len(after),
        out_specs=[pl.BlockSpec((rows, width + 128), lambda k: (0, 0))] * many,
        out_shape=[jax.ShapeDtypeStruct((rows, width + 128), BF16)] * many,
        scratch_shapes=[
            pltpu.VMEM((length, 2 * HEAD_WIDTH), BF16),
            pltpu.VMEM((many, rows, 128), F32),
        ],
        compiler_params=params(40),
        cost_estimate=pl.CostEstimate(
            flops=8 * many * rows * width * length,
            bytes_accessed=4 * length * width // 8 + 4 * many * rows * width,
            transcendentals=many * rows * width // HEAD_WIDTH * length,
        ),
        name="prefix_attention",
    )(*queries, keys, values, *after)


def merged(stats, parts, count):
    top = functools.reduce(jnp.maximum, stats)
    weights = [jnp.exp2(s - top) for s in stats]
    total = functools.reduce(jnp.add, weights)
    shares = [w / total for w in weights]
    out = []
    for h in range(count):
        out.append(
            functools.reduce(jnp.add, [w[:, h : h + 1] * part(h) for w, part in zip(shares, parts)])
        )
    return out, top + jnp.log2(total)


def merge_kernel(*refs):
    ins, out_ref = refs[:-1], refs[-1]
    width = out_ref.shape[1] - 128
    stats = [decode(r[:, width:]) for r in ins]
    parts = [
        lambda h, r=r: r[:, h * HEAD_WIDTH : (h + 1) * HEAD_WIDTH].astype(F32) for r in ins
    ]
    out, stat = merged(stats, parts, width // HEAD_WIDTH)
    for h, x in enumerate(out):
        out_ref[:, h * HEAD_WIDTH : (h + 1) * HEAD_WIDTH] = x.astype(BF16)
    lane = lanes(stat.shape)
    stat = jnp.where(lane < STAT, stat, 0.0)
    stat = stat + pltpu.roll(stat, STAT, 1) + pltpu.roll(stat, 2 * STAT, 1)
    out_ref[:, width:] = encode(stat)


def merge(*messages):
    first = messages[0]
    return pl.pallas_call(
        merge_kernel,
        out_shape=jax.ShapeDtypeStruct(first.shape, BF16),
        compiler_params=params(24),
        cost_estimate=pl.CostEstimate(
            flops=first.size * 4, bytes_accessed=first.size * 2 * (len(messages) + 1), transcendentals=0
        ),
        name="merge_partials",
    )(*messages)


def outgoing_kernel(prompt_ref, q_ref, out_ref):
    rows, slots = q_ref.shape[0], out_ref.shape[0]
    prompt = prompt_ref[...]
    across = jnp.broadcast_to(prompt, (rows, rows))
    first = lax.broadcasted_iota(jnp.int32, (rows, rows), 0) < lanes((rows, rows))
    earlier = (across.T == across) & first
    arrival = jnp.sum(earlier.astype(jnp.int32), axis=0, keepdims=True)
    slot = lax.broadcasted_iota(jnp.int32, (slots, rows), 0)
    wanted = (slot // (2 * CAP) == prompt) & (slot % CAP == arrival)
    chooser = jnp.where(wanted, 1.0, 0.0).astype(BF16)
    out_ref[...] = jnp.dot(chooser, q_ref[...], preferred_element_type=F32).astype(BF16)


def outgoing_part(row_prompt, queries, slots):
    rows, width = queries.shape
    whole = lambda shape: pl.BlockSpec(shape, lambda i: (0, i))
    return pl.pallas_call(
        outgoing_kernel,
        grid=(4,),
        in_specs=[pl.BlockSpec((1, rows), lambda i: (0, 0)), whole((rows, width // 4))],
        out_specs=whole((slots, width // 4)),
        out_shape=jax.ShapeDtypeStruct((slots, width), BF16),
        compiler_params=params(16),
        name="outgoing_queries",
    )(row_prompt[None, :], queries)


def suffix_kernel(length_ref, slot_ref, q_ref, k_ref, v_ref, mean_ref, stat_ref):
    heads = KEY_HEADS * HEADS_PER_KEY
    rows = q_ref.shape[0]
    shape = (heads, KEY_HEADS * HEAD_WIDTH)
    mine = lanes(shape) // HEAD_WIDTH == lax.broadcasted_iota(jnp.int32, shape, 0) // HEADS_PER_KEY
    square = lanes((heads, 128)) == lax.broadcasted_iota(jnp.int32, (heads, 128), 0)
    for i in range(rows):
        row = pl.program_id(0) * rows + i
        slot = slot_ref[row]
        q = jnp.concatenate([q_ref[i]] * KEY_HEADS, axis=1)
        q = jnp.where(mine, q, jnp.zeros_like(q))
        scores = lax.dot_general(
            q, k_ref[i], (((1,), (1,)), ((), ())), preferred_element_type=F32
        )
        seen = lanes(scores.shape) < length_ref[row]
        scores = jnp.where(seen, scores * SCALE, -jnp.inf)
        top = jnp.max(scores, axis=1, keepdims=True)
        weights = jnp.exp2(scores - top).astype(BF16)
        total = jnp.sum(weights.astype(F32), axis=1, keepdims=True)
        blend = jnp.dot(weights, v_ref[i], preferred_element_type=F32)
        for k in range(KEY_HEADS):
            part = slice(k * HEADS_PER_KEY, (k + 1) * HEADS_PER_KEY)
            mean_ref[slot, part, :] = (
                blend[part, k * HEAD_WIDTH : (k + 1) * HEAD_WIDTH] / total[part]
            )
        level = top + jnp.log2(total)
        stat_ref[slot] = jnp.sum(jnp.where(square, level, 0.0), axis=0, keepdims=True)


def suffix_part(queries, keys, values, length, slot, step=4):
    rows, width = queries.shape
    heads = width // HEAD_WIDTH
    entry = pl.BlockSpec((step,) + keys.shape[1:], lambda r, *_: (r, 0, 0))
    return pl.pallas_call(
        suffix_kernel,
        grid_spec=pltpu.PrefetchScalarGridSpec(
            num_scalar_prefetch=2,
            grid=(rows // step,),
            in_specs=[
                pl.BlockSpec((step, heads, HEAD_WIDTH), lambda r, *_: (r, 0, 0)),
                entry,
                entry,
            ],
            out_specs=[
                pl.BlockSpec((rows, heads, HEAD_WIDTH), lambda r, *_: (0, 0, 0)),
                pl.BlockSpec((rows, 1, 128), lambda r, *_: (0, 0, 0)),
            ],
        ),
        out_shape=[
            jax.ShapeDtypeStruct((rows, heads, HEAD_WIDTH), F32),
            jax.ShapeDtypeStruct((rows, 1, 128), F32),
        ],
        compiler_params=params(58),
        cost_estimate=pl.CostEstimate(
            flops=2 * keys.size * heads * 2,
            bytes_accessed=keys.size * 4,
            transcendentals=rows * heads * keys.shape[1],
        ),
        name="suffix_attention",
    )(length, slot, queries.reshape(rows, heads, HEAD_WIDTH), keys, values)


def final_kernel(*refs):
    arrived, (pick_ref, mean_ref, stat_ref, out_ref) = refs[:-4], refs[-4:]
    for group, ref in enumerate(arrived):
        width = ref.shape[1] - 128
        count = width // HEAD_WIDTH
        stats, parts = [], []
        for half in range(2):
            chosen = jnp.dot(pick_ref[half], ref[...], preferred_element_type=F32)
            stats.append(decode(chosen[:, width:]))
            parts.append(lambda h, c=chosen: c[:, h * HEAD_WIDTH : (h + 1) * HEAD_WIDTH])
        base = group * width
        stat = stat_ref[:, 0, :]
        if group:
            stat = pltpu.roll(stat, 128 - group * count, 1)
        stats.append(stat)
        parts.append(
            lambda h: mean_ref[:, group * count + h, :]
        )
        out, _ = merged(stats, parts, count)
        for h, x in enumerate(out):
            out_ref[:, base + h * HEAD_WIDTH : base + (h + 1) * HEAD_WIDTH] = x.astype(BF16)


def final_part(arrived, pick, mean, stat):
    return pl.pallas_call(
        final_kernel,
        out_shape=jax.ShapeDtypeStruct((mean.shape[0], mean.shape[1] * mean.shape[2]), BF16),
        compiler_params=params(24),
        name="last_merge",
    )(*arrived, pick, mean, stat)


def swapped(x, turn):
    pairs = {"near": [1, 0, 3, 2], "next": [3, 2, 1, 0], "far": [2, 3, 0, 1]}[turn]
    return lax.ppermute(x, "z", list(enumerate(pairs)))


def later(x, after):
    return lax.optimization_barrier((x, after))[0]


def in_plane(x):
    return lax.all_to_all(x, ("prefix", "xh"), split_axis=0, concat_axis=0, tiled=True)


def local(
    queries,
    row_prompt,
    suffix_length,
    result_slot,
    prompt_keys,
    prompt_values,
    continuation_keys,
    continuation_values,
):
    sides = lax.axis_size("xh")
    rows = queries.shape[0]
    slots = lax.axis_size("prefix") * sides * CAP
    whole = in_plane(outgoing_part(row_prompt, queries, slots))
    mean, stat = suffix_part(
        queries, continuation_keys, continuation_values, suffix_length, result_slot
    )
    span = queries.shape[1] // GROUPS
    arrived = [whole[:, g * span : (g + 1) * span] for g in range(GROUPS)]
    indices = jnp.arange(rows)
    earlier = (row_prompt[:, None] == row_prompt[None, :]) & (indices[None, :] < indices[:, None])
    arrival = jnp.sum(earlier.astype(jnp.int32), axis=1)
    slot = jnp.arange(slots)
    wanted = (slot[None, :] // (sides * CAP) == row_prompt[:, None]) & (
        slot[None, :] % CAP == arrival[:, None]
    )
    placer = indices[:, None] == result_slot[None, :]
    taken = jnp.any(placer[:, :, None] & wanted[None], axis=1)
    side = slot // CAP % sides
    pick = jnp.stack([taken & (side == x)[None] for x in range(2)]).astype(BF16)
    keys, values = prompt_keys[0], prompt_values[0]
    attend = lambda group, queries, after: prefix_part(queries, keys, values, group, after)
    near_0, next_0 = swapped(arrived[0], "near"), swapped(arrived[0], "next")
    own_0 = attend(0, [arrived[0]], [stat])
    far_q_0 = swapped(later(arrived[0], own_0), "far")
    own_1 = attend(1, [arrived[1]], own_0)
    source_1 = later(arrived[1], own_1)
    near_1, next_1 = swapped(source_1, "near"), swapped(source_1, "next")
    pair_0 = attend(0, [near_0, next_0], own_1)
    far_q_1 = swapped(later(arrived[1], pair_0), "far")
    back_0 = [swapped(pair_0[0], "near"), swapped(pair_0[1], "next")]
    far_0 = attend(0, [far_q_0], pair_0[:1])
    back_0.append(swapped(far_0[0], "far"))
    pair_1 = attend(1, [near_1, next_1], far_0)
    back_1 = [swapped(pair_1[0], "near"), swapped(pair_1[1], "next")]
    far_1 = attend(1, [far_q_1], pair_1[:1])
    back_1.append(swapped(far_1[0], "far"))
    back_0 = later(back_0, far_1)
    returned = [
        in_plane(merge(own_0[0], *back_0)),
        in_plane(merge(own_1[0], *back_1)),
    ]
    return final_part(returned, pick, mean, stat)


def solution(mesh):
    fine = Mesh(mesh.devices.reshape(mesh.devices.shape[0], -1, Z), ("prefix", "xh", "z"))
    rows = ("prefix", "xh", "z")
    blocks = ("xh", "z")
    in_specs = (
        P(rows, None),
        P(rows),
        P(rows),
        P(rows),
        P("prefix", blocks, None),
        P("prefix", blocks, None),
        P(rows, None, None),
        P(rows, None, None),
    )
    return jax.shard_map(
        local, mesh=fine, in_specs=in_specs, out_specs=P(rows, None), check_vma=False
    )
```

time: 388 us -> 158 us (0.41)
  waiting for transfers between devices: 147 us -> 33.7 us
  matrix products: 97 us -> 0 us
  Pallas kernels: 0 us -> 70.2 us
  local copies, waits for them, and re-layouts: 72.3 us -> 12.3 us
  other arithmetic: 34.8 us -> 0.42 us
  starting transfers between devices: 34 us -> 41 us
    dot_general x23 -> x0, matrix products: 97 us -> none  [the longest x8 42 us: prefix_block(): jnp.einsum('nkgd,tkd->nkgt', per_head, key_entries, preferred_element_typ...]
    ppermute x7 -> x12, waiting for transfers between devices: 100 us -> 17.5 us  [swapped(): return lax.ppermute(x, 'z', list(enumerate(pairs)))]
    pallas_call x0 -> x11, Pallas kernels: none -> 70.2 us  [the longest x6 54.5 us: prefix_part(): pl.pallas_call(functools.partial(prefix_kernel, rows, many), grid=(count,...]
    reduce_sum x9 -> x0, other arithmetic: 31.5 us -> none  [settle(): weight_sum = jnp.sum(weights.astype(jnp.float32), axis=-1)]
    all_to_all x4 -> x3, waiting for transfers between devices: 46.4 us -> 16.2 us  [in_plane(): lax.all_to_all(x, ('prefix', 'xh'), split_axis=0, concat_axis=0, tiled=True)]
    dynamic_update_slice x24 -> x0, local copies, waits for them, and re-layouts: 16.2 us -> none  [deposit(): lax.dynamic_update_slice_in_dim(whole, piece_new, offset, 0)]
    reshape x8 -> x0, local copies, waits for them, and re-layouts: 15.6 us -> none  [the longest x1 7.63 us: to_owner(): tensor = tensor.reshape(members, groups, CAP, -1)]
    while x32 -> x0, local copies, waits for them, and re-layouts: 14.1 us -> none  [the longest x4 13.1 us: local(): _, collected = lax.fori_loop(1, members, turn, (query_group_block, started))]
  transfers between devices with their start and end apart: 11 -> 15, of which waited for: 9 -> 6; matrix products, arithmetic and copies ran while one was open for 15% -> 1% of each run, Pallas kernels for 0% -> 43%
where the time goes in v1:
time: 158 us
  Pallas kernels  70.2 us (44%)
  starting transfers between devices  41 us (26%)
  waiting for transfers between devices  33.7 us (21%)
  local copies, waits for them, and re-layouts  12.3 us (8%)
    pallas_call x6, Pallas kernels, prefix_part(): pl.pallas_call(functools.partial(prefix_kernel, rows, many), grid=(count,...  54.5 us
    all_to_all x3, starting transfers between devices, in_plane(): lax.all_to_all(x, ('prefix', 'xh'), split_axis=0, concat_axis=0, tiled=True)  24.8 us
    ppermute x12, waiting for transfers between devices, swapped(): return lax.ppermute(x, 'z', list(enumerate(pairs)))  17.5 us
    all_to_all x3, waiting for transfers between devices, in_plane(): lax.all_to_all(x, ('prefix', 'xh'), split_axis=0, concat_axis=0, tiled=True)  16.2 us
    ppermute x12, starting transfers between devices, swapped(): return lax.ppermute(x, 'z', list(enumerate(pairs)))  16.2 us
    pallas_call x1, Pallas kernels, suffix_part(): pl.pallas_call(suffix_kernel, grid_spec=pltpu.PrefetchScalarGridSpec(num_...  10.1 us
    unnamed x19, local copies, waits for them, and re-layouts  6.75 us
    all_to_all x6, local copies, waits for them, and re-layouts, in_plane(): lax.all_to_all(x, ('prefix', 'xh'), split_axis=0, concat_axis=0, tiled=True)  5.44 us
  transfers between devices with their start and end apart: 15, of which 6 were waited for; matrix products, arithmetic and copies ran while one was open for 1% of the time, Pallas kernels for 43%

profile of v1, /device:TPU:1, one launch (start us, length us, event | category | flops | bytes accessed | tf_op | source)
XLA Modules:
  0.0 157.8 jit_solution(4018504652534385704)
XLA Ops:
  1.6 1.2 outgoing_queries.1
  2.8 1.5 all_to_all.22
  4.3 8.6 %all-to-all-start = ((bf16[32,2,8192]{2,1,0:T(2,128)(2,1)}), bf16[32,2,8192]{2,1,0:T(2,128)(2,1)S(1)}, u32[]{:S(2)}, u32[]{:S(2)}) async-start(bf16[32,2,8192]{2,1,0:T(2,128)(2,1)} %all_to_all.22), calls=%async_computation | async-start | bytes 2097152 | tf_op jit(solution)/shard_map/all_to_all | solution.py:307
  13.7 10.1 %suffix_attention.1 = (f32[16,64,128]{2,1,0:T(8,128)}, f32[16,1,128]{2,1,0:T(1,128)}) custom-call(s32[16]{0:T(128)} %length_ref.1, s32[16]{0:T(128)} %slot_ref.1, bf16[16,64,128]{2,1,0:T(8,128)(2,1)} %bitcast.22, bf16[16,128,1024]{2,1,0:T(8,128)(2,1)} %k_ref.1, bf16[16,128,1024]{2,1,0:T(8,128)(2,1)} %v_ref.1), custom_call_target="tpu_custom_call" | custom-call | flops 536870912 | bytes 8388608 | tf_op jit(solution)/shard_map/suffix_attention/pallas_call | solution.py:236
  23.9 5.9 %all-to-all-done = bf16[32,2,8192]{2,1,0:T(2,128)(2,1)S(1)} async-done(((bf16[32,2,8192]{2,1,0:T(2,128)(2,1)}), bf16[32,2,8192]{2,1,0:T(2,128)(2,1)S(1)}, u32[]{:S(2)}, u32[]{:S(2)}) %all-to-all-start) | async-done | bytes 1048608 | tf_op jit(solution)/shard_map/all_to_all | solution.py:307
  30.4 1.7 %collective-permute-start = (bf16[64,4096]{1,0:T(8,128)(2,1)S(1)}, bf16[64,4096]{1,0:T(8,128)(2,1)S(1)}, u32[]{:S(2)}, u32[]{:S(2)}) collective-permute-start(bf16[64,4096]{1,0:T(8,128)(2,1)S(1)} %get-tuple-element.20.refs_0_), channel_id=1, source_target_pairs={{0,1},{1,0},{2,3},{3,2},{4,5},{5,4},{6,7},{7,6},{8,9},{9,8},{10,11... | collective-permute-start | bytes 1572872 | tf_op jit(solution)/shard_map/ppermute | solution.py:299
  32.1 2.2 %collective-permute-start.1 = (bf16[64,4096]{1,0:T(8,128)(2,1)S(1)}, bf16[64,4096]{1,0:T(8,128)(2,1)S(1)}, u32[]{:S(2)}, u32[]{:S(2)}) collective-permute-start(bf16[64,4096]{1,0:T(8,128)(2,1)S(1)} %get-tuple-element.20.refs_0_), channel_id=1, source_target_pairs={{0,3},{1,2},{2,1},{3,0},{4,7},{5,6},{6,5},{7,4},{8,11},{9,10},{10,... | collective-permute-start | bytes 1572872 | tf_op jit(solution)/shard_map/ppermute | solution.py:299
  34.3 2.2 %copy-done.6 = bf16[1,2048,1024]{2,1,0:T(8,128)(2,1)S(1)} copy-done((bf16[1,2048,1024]{2,1,0:T(8,128)(2,1)S(1)}, bf16[1,2048,1024]{2,1,0:T(8,128)(2,1)}, u32[]{:S(2)}) %copy-start.6) | copy-done | bytes 4194328
  36.5 2.2 %copy-done.7 = bf16[1,2048,1024]{2,1,0:T(8,128)(2,1)S(1)} copy-done((bf16[1,2048,1024]{2,1,0:T(8,128)(2,1)S(1)}, bf16[1,2048,1024]{2,1,0:T(8,128)(2,1)}, u32[]{:S(2)}) %copy-start.7) | copy-done | bytes 4194328
  38.7 7.1 %prefix_attention.6.refs_3_.refs_0_ = bf16[64,4224]{1,0:T(8,128)(2,1)S(1)} custom-call(bf16[64,4096]{1,0:T(8,128)(2,1)S(1)} %get-tuple-element.20.refs_0_, bf16[2048,1024]{1,0:T(8,128)(2,1)S(1)} %bitcast.10, bf16[2048,1024]{1,0:T(8,128)(2,1)S(1)} %bitcast.16, f32[16,1,128]{2,1,0:T(1,128)S(1)} %copy-done.3), custom_call_target="tpu_custom_call" | custom-call | flops 4294967296 | bytes 5242880 | tf_op jit(solution)/shard_map/prefix_attention/pallas_call | solution.py:112
  45.8 7.1 %prefix_attention.7.refs_4_.refs_0_ = bf16[64,4224]{1,0:T(8,128)(2,1)S(1)} custom-call(bf16[64,4096]{1,0:T(8,128)(2,1)S(1)} %get-tuple-element.22.refs_0_, bf16[2048,1024]{1,0:T(8,128)(2,1)S(1)} %bitcast.11, bf16[2048,1024]{1,0:T(8,128)(2,1)S(1)} %bitcast.17, bf16[64,4224]{1,0:T(8,128)(2,1)S(1)} %prefix_attention.6.refs_3_.refs_0_), custom_call_target="tpu_custom_call" | custom-call | flops 4294967296 | bytes 5242880 | tf_op jit(solution)/shard_map/prefix_attention/pallas_call | solution.py:112
  54.4 1.9 %collective-permute-start.4 = (bf16[64,4096]{1,0:T(8,128)(2,1)S(1)}, bf16[64,4096]{1,0:T(8,128)(2,1)S(1)}, u32[]{:S(2)}, u32[]{:S(2)}) collective-permute-start(bf16[64,4096]{1,0:T(8,128)(2,1)S(1)} %get-tuple-element.20.refs_0_), channel_id=1, source_target_pairs={{0,2},{1,3},{2,0},{3,1},{4,6},{5,7},{6,4},{7,5},{8,10},{9,11},{10,... | collective-permute-start | bytes 1572872 | tf_op jit(solution)/shard_map/ppermute | solution.py:299
  56.3 12.2 %prefix_attention.8 = (bf16[64,4224]{1,0:T(8,128)(2,1)S(1)}, bf16[64,4224]{1,0:T(8,128)(2,1)S(1)}) custom-call(bf16[64,4096]{1,0:T(8,128)(2,1)S(1)} %collective-permute-done.refs_0_, bf16[64,4096]{1,0:T(8,128)(2,1)S(1)} %collective-permute-done.1.refs_1_, bf16[2048,1024]{1,0:T(8,128)(2,1)S(1)} %bitcast.12, bf16[2048,1024]{1,0:T(8,128)(2,1)S(1)} %bitcast.18, ...), custom_call_target="tpu_custom_call" | custom-call | flops 8589934592 | bytes 6291456 | tf_op jit(solution)/shard_map/prefix_attention/pallas_call | solution.py:112
  69.9 6.6 %collective-permute-done.4.refs_0_ = bf16[64,4096]{1,0:T(8,128)(2,1)S(1)} collective-permute-done((bf16[64,4096]{1,0:T(8,128)(2,1)S(1)}, bf16[64,4096]{1,0:T(8,128)(2,1)S(1)}, u32[]{:S(2)}, u32[]{:S(2)}) %collective-permute-start.4) | collective-permute-done | bytes 524320 | tf_op jit(solution)/shard_map/ppermute | solution.py:299
  76.5 2.1 %collective-permute-start.6 = (bf16[64,4096]{1,0:T(8,128)(2,1)S(1)}, bf16[64,4096]{1,0:T(8,128)(2,1)S(1)}, u32[]{:S(2)}, u32[]{:S(2)}) collective-permute-start(bf16[64,4096]{1,0:T(8,128)(2,1)S(1)} %get-tuple-element.22.refs_0_), channel_id=1, source_target_pairs={{0,2},{1,3},{2,0},{3,1},{4,6},{5,7},{6,4},{7,5},{8,10},{9,11},{10,... | collective-permute-start | bytes 1572872 | tf_op jit(solution)/shard_map/ppermute | solution.py:299
  78.6 7.1 %prefix_attention.9.refs_4_ = bf16[64,4224]{1,0:T(8,128)(2,1)S(1)} custom-call(bf16[64,4096]{1,0:T(8,128)(2,1)S(1)} %collective-permute-done.4.refs_0_, bf16[2048,1024]{1,0:T(8,128)(2,1)S(1)} %bitcast.13, bf16[2048,1024]{1,0:T(8,128)(2,1)S(1)} %bitcast.19, bf16[64,4224]{1,0:T(8,128)(2,1)S(1)} %get-tuple-element.18.refs_3_), custom_call_target="tpu_custom_call" | custom-call | flops 4294967296 | bytes 5242880 | tf_op jit(solution)/shard_map/prefix_attention/pallas_call | solution.py:112
  86.7 13.1 %prefix_attention.10 = (bf16[64,4224]{1,0:T(8,128)(2,1)}, bf16[64,4224]{1,0:T(8,128)(2,1)}) custom-call(bf16[64,4096]{1,0:T(8,128)(2,1)S(1)} %collective-permute-done.7.refs_0_, bf16[64,4096]{1,0:T(8,128)(2,1)S(1)} %collective-permute-done.8.refs_1_, bf16[2048,1024]{1,0:T(8,128)(2,1)S(1)} %bitcast.14, bf16[2048,1024]{1,0:T(8,128)(2,1)S(1)} %bitcast.20, ...), custom_call_target="tpu_custom_call" | custom-call | flops 8589934592 | bytes 6291456 | tf_op jit(solution)/shard_map/prefix_attention/pallas_call | solution.py:112
  99.8 2.2 %collective-permute-start.10 = (bf16[64,4224]{1,0:T(8,128)(2,1)}, bf16[64,4224]{1,0:T(8,128)(2,1)S(1)}, u32[]{:S(2)}, u32[]{:S(2)}) collective-permute-start(bf16[64,4224]{1,0:T(8,128)(2,1)} %get-tuple-element.27), channel_id=1, source_target_pairs={{0,3},{1,2},{2,1},{3,0},{4,7},{5,6},{6,5},{7,4},{8,11},{9,10},{10,... | collective-permute-start | bytes 1622024 | tf_op jit(solution)/shard_map/ppermute | solution.py:299
  102.0 7.9 %prefix_attention.11 = bf16[64,4224]{1,0:T(8,128)(2,1)} custom-call(bf16[64,4096]{1,0:T(8,128)(2,1)S(1)} %collective-permute-done.6.refs_0_, bf16[2048,1024]{1,0:T(8,128)(2,1)S(1)} %bitcast.15, bf16[2048,1024]{1,0:T(8,128)(2,1)S(1)} %bitcast.21, bf16[64,4224]{1,0:T(8,128)(2,1)} %get-tuple-element.23.refs_3_), custom_call_target="tpu_custom_call" | custom-call | flops 4294967296 | bytes 5242880 | tf_op jit(solution)/shard_map/prefix_attention/pallas_call | solution.py:112
  109.9 1.0 collective-permute-done.5.refs_3_
  110.9 2.1 %collective-permute-start.11 = (bf16[64,4224]{1,0:T(8,128)(2,1)}, bf16[64,4224]{1,0:T(8,128)(2,1)S(1)}, u32[]{:S(2)}, u32[]{:S(2)}) collective-permute-start(bf16[64,4224]{1,0:T(8,128)(2,1)} %prefix_attention.11), channel_id=1, source_target_pairs={{0,2},{1,3},{2,0},{3,1},{4,6},{5,7},{6,4},{7,5},{8,10},{9,11},{10,... | collective-permute-start | bytes 1622024 | tf_op jit(solution)/shard_map/ppermute | solution.py:299
  113.1 1.4 merge_partials.2
  114.4 1.0 all_to_all.25
  115.5 8.8 %all-to-all-start.1 = ((bf16[32,2,4224]{2,1,0:T(2,128)(2,1)}), bf16[32,2,4224]{2,1,0:T(2,128)(2,1)}, u32[]{:S(2)}, u32[]{:S(2)}) async-start(bf16[32,2,4224]{2,1,0:T(2,128)(2,1)} %all_to_all.25), calls=%async_computation.1 | async-start | bytes 1081344 | tf_op jit(solution)/shard_map/all_to_all | solution.py:307
  124.4 2.1 %collective-permute-done.10.refs_2_ = bf16[64,4224]{1,0:T(8,128)(2,1)S(1)} collective-permute-done((bf16[64,4224]{1,0:T(8,128)(2,1)}, bf16[64,4224]{1,0:T(8,128)(2,1)S(1)}, u32[]{:S(2)}, u32[]{:S(2)}) %collective-permute-start.10) | collective-permute-done | bytes 540704 | tf_op jit(solution)/shard_map/ppermute | solution.py:299
  126.4 7.8 %collective-permute-done.11.refs_3_ = bf16[64,4224]{1,0:T(8,128)(2,1)S(1)} collective-permute-done((bf16[64,4224]{1,0:T(8,128)(2,1)}, bf16[64,4224]{1,0:T(8,128)(2,1)S(1)}, u32[]{:S(2)}, u32[]{:S(2)}) %collective-permute-start.11) | collective-permute-done | bytes 540704 | tf_op jit(solution)/shard_map/ppermute | solution.py:299
  134.3 1.4 merge_partials.3
  135.6 1.0 all_to_all.28
  136.7 7.4 %all-to-all-start.2 = ((bf16[32,2,4224]{2,1,0:T(2,128)(2,1)}), bf16[32,2,4224]{2,1,0:T(2,128)(2,1)S(1)}, u32[]{:S(2)}, u32[]{:S(2)}) async-start(bf16[32,2,4224]{2,1,0:T(2,128)(2,1)} %all_to_all.28), calls=%async_computation.2 | async-start | bytes 1081344 | tf_op jit(solution)/shard_map/all_to_all | solution.py:307
  144.3 1.3 all_to_all.27.refs_0_
  145.5 10.3 %all-to-all-done.2 = bf16[32,2,4224]{2,1,0:T(2,128)(2,1)S(1)} async-done(((bf16[32,2,4224]{2,1,0:T(2,128)(2,1)}), bf16[32,2,4224]{2,1,0:T(2,128)(2,1)S(1)}, u32[]{:S(2)}, u32[]{:S(2)}) %all-to-all-start.2) | async-done | bytes 540704 | tf_op jit(solution)/shard_map/all_to_all | solution.py:307
  156.1 1.7 %last_merge.1 = bf16[16,8192]{1,0:T(8,128)(2,1)} custom-call(bf16[64,4224]{1,0:T(8,128)(2,1)S(1)} %all_to_all.27.refs_0_, bf16[64,4224]{1,0:T(8,128)(2,1)S(1)} %all_to_all.30.refs_1_, bf16[2,16,64]{2,1,0:T(8,128)(2,1)S(1)} %add_convert_fusion.refs_2_, f32[16,64,128]{2,1,0:T(8,128)S(1)} %copy-done.2, f32[16,1,128]{2,1,0:T(1,128)S(1)} %copy-done.3), custom_call_target="tpu_custom_call" | custom-call | tf_op jit(solution)/shard_map/last_merge/pallas_call | solution.py:289
  (43 shorter events, 7.3 us)
Async XLA Ops:
  0.0 0.9 copy-start
  1.0 0.7 copy-start.4
  1.6 11.3 %copy-start.1 = (bf16[16,8192]{1,0:T(8,128)(2,1)S(1)}, bf16[16,8192]{1,0:T(8,128)(2,1)}, u32[]{:S(2)}) copy-start(bf16[16,8192]{1,0:T(8,128)(2,1)} %q_ref.1) | copy-start | bytes 786436
  4.3 25.5 %all-to-all-start = ((bf16[32,2,8192]{2,1,0:T(2,128)(2,1)}), bf16[32,2,8192]{2,1,0:T(2,128)(2,1)S(1)}, u32[]{:S(2)}, u32[]{:S(2)}) async-start(bf16[32,2,8192]{2,1,0:T(2,128)(2,1)} %all_to_all.22), calls=%async_computation | async-start | bytes 2097152 | tf_op jit(solution)/shard_map/all_to_all | solution.py:307
  13.7 10.1 %copy-start.5 = (s32[16]{0:T(128)S(1)}, s32[16]{0:T(128)}, u32[]{:S(2)}) copy-start(s32[16]{0:T(128)} %param.9) | copy-start | bytes 196
  23.8 10.6 %copy-start.3 = (f32[16,1,128]{2,1,0:T(1,128)S(1)}, f32[16,1,128]{2,1,0:T(1,128)}, u32[]{:S(2)}) copy-start(f32[16,1,128]{2,1,0:T(1,128)} %get-tuple-element.17.refs_3_.refs_4_) | copy-start | bytes 24580
  30.4 25.9 %collective-permute-start = (bf16[64,4096]{1,0:T(8,128)(2,1)S(1)}, bf16[64,4096]{1,0:T(8,128)(2,1)S(1)}, u32[]{:S(2)}, u32[]{:S(2)}) collective-permute-start(bf16[64,4096]{1,0:T(8,128)(2,1)S(1)} %get-tuple-element.20.refs_0_), channel_id=1, source_target_pairs={{0,1},{1,0},{2,3},{3,2},{4,5},{5,4},{6,7},{7,6},{8,9},{9,8},{10,11... | collective-permute-start | bytes 1572872 | tf_op jit(solution)/shard_map/ppermute | solution.py:299
  32.1 24.2 %collective-permute-start.1 = (bf16[64,4096]{1,0:T(8,128)(2,1)S(1)}, bf16[64,4096]{1,0:T(8,128)(2,1)S(1)}, u32[]{:S(2)}, u32[]{:S(2)}) collective-permute-start(bf16[64,4096]{1,0:T(8,128)(2,1)S(1)} %get-tuple-element.20.refs_0_), channel_id=1, source_target_pairs={{0,3},{1,2},{2,1},{3,0},{4,7},{5,6},{6,5},{7,4},{8,11},{9,10},{10,... | collective-permute-start | bytes 1572872 | tf_op jit(solution)/shard_map/ppermute | solution.py:299
  34.3 2.2 %copy-start.6 = (bf16[1,2048,1024]{2,1,0:T(8,128)(2,1)S(1)}, bf16[1,2048,1024]{2,1,0:T(8,128)(2,1)}, u32[]{:S(2)}) copy-start(bf16[1,2048,1024]{2,1,0:T(8,128)(2,1)} %param.12) | copy-start | bytes 12582916
  36.5 2.2 %copy-start.7 = (bf16[1,2048,1024]{2,1,0:T(8,128)(2,1)S(1)}, bf16[1,2048,1024]{2,1,0:T(8,128)(2,1)}, u32[]{:S(2)}) copy-start(bf16[1,2048,1024]{2,1,0:T(8,128)(2,1)} %param.13) | copy-start | bytes 12582916
  52.9 32.8 %collective-permute-start.7 = (bf16[64,4096]{1,0:T(8,128)(2,1)S(1)}, bf16[64,4096]{1,0:T(8,128)(2,1)S(1)}, u32[]{:S(2)}, u32[]{:S(2)}) collective-permute-start(bf16[64,4096]{1,0:T(8,128)(2,1)S(1)} %get-tuple-element.22.refs_0_), channel_id=1, source_target_pairs={{0,1},{1,0},{2,3},{3,2},{4,5},{5,4},{6,7},{7,6},{8,9},{9,8},{10,11... | collective-permute-start | bytes 1572872 | tf_op jit(solution)/shard_map/ppermute | solution.py:299
  53.8 32.9 %collective-permute-start.8 = (bf16[64,4096]{1,0:T(8,128)(2,1)S(1)}, bf16[64,4096]{1,0:T(8,128)(2,1)S(1)}, u32[]{:S(2)}, u32[]{:S(2)}) collective-permute-start(bf16[64,4096]{1,0:T(8,128)(2,1)S(1)} %get-tuple-element.22.refs_0_), channel_id=1, source_target_pairs={{0,3},{1,2},{2,1},{3,0},{4,7},{5,6},{6,5},{7,4},{8,11},{9,10},{10,... | collective-permute-start | bytes 1572872 | tf_op jit(solution)/shard_map/ppermute | solution.py:299
  54.4 22.1 %collective-permute-start.4 = (bf16[64,4096]{1,0:T(8,128)(2,1)S(1)}, bf16[64,4096]{1,0:T(8,128)(2,1)S(1)}, u32[]{:S(2)}, u32[]{:S(2)}) collective-permute-start(bf16[64,4096]{1,0:T(8,128)(2,1)S(1)} %get-tuple-element.20.refs_0_), channel_id=1, source_target_pairs={{0,2},{1,3},{2,0},{3,1},{4,6},{5,7},{6,4},{7,5},{8,10},{9,11},{10,... | collective-permute-start | bytes 1572872 | tf_op jit(solution)/shard_map/ppermute | solution.py:299
  68.4 44.6 %collective-permute-start.2 = (bf16[64,4224]{1,0:T(8,128)(2,1)S(1)}, bf16[64,4224]{1,0:T(8,128)(2,1)S(1)}, u32[]{:S(2)}, u32[]{:S(2)}) collective-permute-start(bf16[64,4224]{1,0:T(8,128)(2,1)S(1)} %get-tuple-element.18.refs_3_), channel_id=1, source_target_pairs={{0,1},{1,0},{2,3},{3,2},{4,5},{5,4},{6,7},{7,6},{8,9},{9,8},{10,11... | collective-permute-start | bytes 1622024 | tf_op jit(solution)/shard_map/ppermute | solution.py:299
  69.3 43.8 %collective-permute-start.3 = (bf16[64,4224]{1,0:T(8,128)(2,1)S(1)}, bf16[64,4224]{1,0:T(8,128)(2,1)S(1)}, u32[]{:S(2)}, u32[]{:S(2)}) collective-permute-start(bf16[64,4224]{1,0:T(8,128)(2,1)S(1)} %get-tuple-element.19), channel_id=1, source_target_pairs={{0,3},{1,2},{2,1},{3,0},{4,7},{5,6},{6,5},{7,4},{8,11},{9,10},{10,... | collective-permute-start | bytes 1622024 | tf_op jit(solution)/shard_map/ppermute | solution.py:299
  76.5 25.6 %collective-permute-start.6 = (bf16[64,4096]{1,0:T(8,128)(2,1)S(1)}, bf16[64,4096]{1,0:T(8,128)(2,1)S(1)}, u32[]{:S(2)}, u32[]{:S(2)}) collective-permute-start(bf16[64,4096]{1,0:T(8,128)(2,1)S(1)} %get-tuple-element.22.refs_0_), channel_id=1, source_target_pairs={{0,2},{1,3},{2,0},{3,1},{4,6},{5,7},{6,4},{7,5},{8,10},{9,11},{10,... | collective-permute-start | bytes 1572872 | tf_op jit(solution)/shard_map/ppermute | solution.py:299
  85.7 25.2 %collective-permute-start.5 = (bf16[64,4224]{1,0:T(8,128)(2,1)S(1)}, bf16[64,4224]{1,0:T(8,128)(2,1)S(1)}, u32[]{:S(2)}, u32[]{:S(2)}) collective-permute-start(bf16[64,4224]{1,0:T(8,128)(2,1)S(1)} %prefix_attention.9.refs_4_), channel_id=1, source_target_pairs={{0,2},{1,3},{2,0},{3,1},{4,6},{5,7},{6,4},{7,5},{8,10},{9,11},{10,... | collective-permute-start | bytes 1622024 | tf_op jit(solution)/shard_map/ppermute | solution.py:299
  99.8 26.6 %collective-permute-start.10 = (bf16[64,4224]{1,0:T(8,128)(2,1)}, bf16[64,4224]{1,0:T(8,128)(2,1)S(1)}, u32[]{:S(2)}, u32[]{:S(2)}) collective-permute-start(bf16[64,4224]{1,0:T(8,128)(2,1)} %get-tuple-element.27), channel_id=1, source_target_pairs={{0,3},{1,2},{2,1},{3,0},{4,7},{5,6},{6,5},{7,4},{8,11},{9,10},{10,... | collective-permute-start | bytes 1622024 | tf_op jit(solution)/shard_map/ppermute | solution.py:299
  102.0 24.4 %collective-permute-start.9 = (bf16[64,4224]{1,0:T(8,128)(2,1)}, bf16[64,4224]{1,0:T(8,128)(2,1)S(1)}, u32[]{:S(2)}, u32[]{:S(2)}) collective-permute-start(bf16[64,4224]{1,0:T(8,128)(2,1)} %get-tuple-element.23.refs_3_), channel_id=1, source_target_pairs={{0,1},{1,0},{2,3},{3,2},{4,5},{5,4},{6,7},{7,6},{8,9},{9,8},{10,11... | collective-permute-start | bytes 1622024 | tf_op jit(solution)/shard_map/ppermute | solution.py:299
  109.9 14.3 %copy-start.8 = (s32[16]{0:T(128)S(1)}, s32[16]{0:T(128)}, u32[]{:S(2)}) copy-start(s32[16]{0:T(128)} %slot_ref.1) | copy-start | bytes 196
  110.9 23.3 %collective-permute-start.11 = (bf16[64,4224]{1,0:T(8,128)(2,1)}, bf16[64,4224]{1,0:T(8,128)(2,1)S(1)}, u32[]{:S(2)}, u32[]{:S(2)}) collective-permute-start(bf16[64,4224]{1,0:T(8,128)(2,1)} %prefix_attention.11), channel_id=1, source_target_pairs={{0,2},{1,3},{2,0},{3,1},{4,6},{5,7},{6,4},{7,5},{8,10},{9,11},{10,... | collective-permute-start | bytes 1622024 | tf_op jit(solution)/shard_map/ppermute | solution.py:299
  115.5 40.6 %copy-start.2 = (f32[16,64,128]{2,1,0:T(8,128)S(1)}, f32[16,64,128]{2,1,0:T(8,128)}, u32[]{:S(2)}) copy-start(f32[16,64,128]{2,1,0:T(8,128)} %get-tuple-element.28.refs_3_) | copy-start | bytes 1572868
  115.5 21.2 %all-to-all-start.1 = ((bf16[32,2,4224]{2,1,0:T(2,128)(2,1)}), bf16[32,2,4224]{2,1,0:T(2,128)(2,1)}, u32[]{:S(2)}, u32[]{:S(2)}) async-start(bf16[32,2,4224]{2,1,0:T(2,128)(2,1)} %all_to_all.25), calls=%async_computation.1 | async-start | bytes 1081344 | tf_op jit(solution)/shard_map/all_to_all | solution.py:307
  136.7 19.2 %all-to-all-start.2 = ((bf16[32,2,4224]{2,1,0:T(2,128)(2,1)}), bf16[32,2,4224]{2,1,0:T(2,128)(2,1)S(1)}, u32[]{:S(2)}, u32[]{:S(2)}) async-start(bf16[32,2,4224]{2,1,0:T(2,128)(2,1)} %all_to_all.28), calls=%async_computation.2 | async-start | bytes 1081344 | tf_op jit(solution)/shard_map/all_to_all | solution.py:307

commit v2 on v1

--- a/solution.py
+++ b/solution.py
@@ -18,8 +18,13 @@
 STAT = 32
 SCALE = HEAD_WIDTH ** (-0.5) * 1.4426950408889634
 MIB = 1024 * 1024
+TUNE = 0.5
 F32 = jnp.float32
 BF16 = jnp.bfloat16
+
+
+def cost(us):
+    return pl.CostEstimate(flops=int(us * 1.15e9), bytes_accessed=0, transcendentals=0)
 
 
 def params(mib):
@@ -46,9 +51,10 @@
     return plane + pltpu.roll(plane, 128 - STAT, 1) + pltpu.roll(plane, 128 - 2 * STAT, 1)
 
 
-def prefix_kernel(rows, many, *refs):
-    q_refs, (k_ref, v_ref) = refs[:many], refs[many : many + 2]
-    out_refs, wide, stat = refs[-2 - many : -2], refs[-2], refs[-1]
+def prefix_kernel(rows, many, split, *refs):
+    q_refs, (k_ref, v_ref) = refs[: 2 * many], refs[2 * many : 2 * many + 2]
+    out_refs, wide, stat = refs[-2 - many * split : -2], refs[-2], refs[-1]
+    share = rows // split
     step = pl.program_id(0)
     width = out_refs[0].shape[1] - 128
 
@@ -67,7 +73,10 @@
         return pl.ds(pl.multiple_of(step * KEY_SPAN + h * HEAD_WIDTH, HEAD_WIDTH), HEAD_WIDTH)
 
     def score(i, first):
-        q = jnp.concatenate([q_refs[i][:, columns(first + j)] for j in range(per_tile)], axis=0)
+        q = jnp.concatenate(
+            [r[:, columns(first + j)] for j in range(per_tile) for r in q_refs[2 * i : 2 * i + 2]],
+            axis=0,
+        )
         return lax.dot_general(
             q, k_ref[...], (((1,), (1,)), ((), ())), preferred_element_type=F32
         )
@@ -89,7 +98,9 @@
             level = old[0] * SCALE + jnp.log2(total)
             for j in range(per_tile):
                 part = slice(j * rows, (j + 1) * rows)
-                out_refs[i][:, columns(first + j)] = mean[part]
+                for n_out in range(split):
+                    rest = j * rows + n_out * share
+                    out_refs[i * split + n_out][:, columns(first + j)] = mean[rest : rest + share]
                 here = lane % STAT == step * HEADS_PER_KEY + first + j
                 gathered[i] = jnp.where(here, level[part], gathered[i])
         scores = ahead
@@ -98,35 +109,33 @@
 
     @pl.when(step == pl.num_programs(0) - 1)
     def _():
-        for i in range(many):
-            out_refs[i][:, width:] = encode(gathered[i])
-
-
-def prefix_part(queries, keys, values, group, after=()):
+        for i in range(many * split):
+            rest = i % split * share
+            out_refs[i][:, width:] = encode(gathered[i // split][rest : rest + share])
+
+
+def prefix_part(queries, keys, values, group, after=(), split=1):
     many = len(queries)
-    rows, width = queries[0].shape
+    queries = [half for block in queries for half in block]
+    rows, width = 2 * queries[0].shape[0], queries[0].shape[1]
     count = width // KEY_SPAN
     length = keys.shape[0]
     entry = pl.BlockSpec((length, HEAD_WIDTH), lambda k: (0, group * count + k))
-    block = pl.BlockSpec((rows, width), lambda k: (0, 0))
-    return pl.pallas_call(
-        functools.partial(prefix_kernel, rows, many),
+    block = pl.BlockSpec((rows // 2, width), lambda k: (0, 0))
+    return pl.pallas_call(
+        functools.partial(prefix_kernel, rows, many, split),
         grid=(count,),
-        in_specs=[block] * many
+        in_specs=[block] * len(queries)
         + [entry, entry]
         + [pl.BlockSpec(memory_space=pl.ANY)] * len(after),
-        out_specs=[pl.BlockSpec((rows, width + 128), lambda k: (0, 0))] * many,
-        out_shape=[jax.ShapeDtypeStruct((rows, width + 128), BF16)] * many,
+        out_specs=[pl.BlockSpec((rows // split, width + 128), lambda k: (0, 0))] * (many * split),
+        out_shape=[jax.ShapeDtypeStruct((rows // split, width + 128), BF16)] * (many * split),
         scratch_shapes=[
             pltpu.VMEM((length, 2 * HEAD_WIDTH), BF16),
             pltpu.VMEM((many, rows, 128), F32),
         ],
         compiler_params=params(40),
-        cost_estimate=pl.CostEstimate(
-            flops=8 * many * rows * width * length,
-            bytes_accessed=4 * length * width // 8 + 4 * many * rows * width,
-            transcendentals=many * rows * width // HEAD_WIDTH * length,
-        ),
+        cost_estimate=cost((1 + 6 * many) * TUNE),
         name="prefix_attention",
     )(*queries, keys, values, *after)
 
@@ -144,8 +153,8 @@
     return out, top + jnp.log2(total)
 
 
-def merge_kernel(*refs):
-    ins, out_ref = refs[:-1], refs[-1]
+def merge_kernel(many, *refs):
+    ins, out_ref = refs[:many], refs[-1]
     width = out_ref.shape[1] - 128
     stats = [decode(r[:, width:]) for r in ins]
     parts = [
@@ -160,17 +169,35 @@
     out_ref[:, width:] = encode(stat)
 
 
-def merge(*messages):
+def merge(messages, after=()):
     first = messages[0]
     return pl.pallas_call(
-        merge_kernel,
+        functools.partial(merge_kernel, len(messages)),
+        in_specs=[pl.BlockSpec(memory_space=pltpu.VMEM)] * len(messages)
+        + [pl.BlockSpec(memory_space=pl.ANY)] * len(after),
         out_shape=jax.ShapeDtypeStruct(first.shape, BF16),
         compiler_params=params(24),
-        cost_estimate=pl.CostEstimate(
-            flops=first.size * 4, bytes_accessed=first.size * 2 * (len(messages) + 1), transcendentals=0
-        ),
+        cost_estimate=cost(1 * TUNE),
         name="merge_partials",
-    )(*messages)
+    )(*messages, *after)
+
+
+def fold_kernel(start, whole_ref, part_ref, out_ref):
+    rows = part_ref.shape[0]
+    rest = slice(rows - start, 2 * rows - start)
+    out_ref[rest] = whole_ref[rest]
+    here = slice(start, start + rows)
+    merge_kernel(2, whole_ref.at[here], part_ref, out_ref.at[here])
+
+
+def fold(whole, part, start):
+    return pl.pallas_call(
+        functools.partial(fold_kernel, start),
+        out_shape=jax.ShapeDtypeStruct(whole.shape, BF16),
+        compiler_params=params(24),
+        cost_estimate=cost(0.1 * TUNE),
+        name="fold_partials",
+    )(whole, part)
 
 
 def outgoing_kernel(prompt_ref, q_ref, out_ref):
@@ -253,11 +280,7 @@
             jax.ShapeDtypeStruct((rows, 1, 128), F32),
         ],
         compiler_params=params(58),
-        cost_estimate=pl.CostEstimate(
-            flops=2 * keys.size * heads * 2,
-            bytes_accessed=keys.size * 4,
-            transcendentals=rows * heads * keys.shape[1],
-        ),
+        cost_estimate=cost(10),
         name="suffix_attention",
     )(length, slot, queries.reshape(rows, heads, HEAD_WIDTH), keys, values)
 
@@ -299,10 +322,6 @@
     return lax.ppermute(x, "z", list(enumerate(pairs)))
 
 
-def later(x, after):
-    return lax.optimization_barrier((x, after))[0]
-
-
 def in_plane(x):
     return lax.all_to_all(x, ("prefix", "xh"), split_axis=0, concat_axis=0, tiled=True)
 
@@ -324,8 +343,6 @@
     mean, stat = suffix_part(
         queries, continuation_keys, continuation_values, suffix_length, result_slot
     )
-    span = queries.shape[1] // GROUPS
-    arrived = [whole[:, g * span : (g + 1) * span] for g in range(GROUPS)]
     indices = jnp.arange(rows)
     earlier = (row_prompt[:, None] == row_prompt[None, :]) & (indices[None, :] < indices[:, None])
     arrival = jnp.sum(earlier.astype(jnp.int32), axis=1)
@@ -338,27 +355,36 @@
     side = slot // CAP % sides
     pick = jnp.stack([taken & (side == x)[None] for x in range(2)]).astype(BF16)
     keys, values = prompt_keys[0], prompt_values[0]
-    attend = lambda group, queries, after: prefix_part(queries, keys, values, group, after)
-    near_0, next_0 = swapped(arrived[0], "near"), swapped(arrived[0], "next")
-    own_0 = attend(0, [arrived[0]], [stat])
-    far_q_0 = swapped(later(arrived[0], own_0), "far")
-    own_1 = attend(1, [arrived[1]], own_0)
-    source_1 = later(arrived[1], own_1)
-    near_1, next_1 = swapped(source_1, "near"), swapped(source_1, "next")
-    pair_0 = attend(0, [near_0, next_0], own_1)
-    far_q_1 = swapped(later(arrived[1], pair_0), "far")
-    back_0 = [swapped(pair_0[0], "near"), swapped(pair_0[1], "next")]
-    far_0 = attend(0, [far_q_0], pair_0[:1])
-    back_0.append(swapped(far_0[0], "far"))
-    pair_1 = attend(1, [near_1, next_1], far_0)
-    back_1 = [swapped(pair_1[0], "near"), swapped(pair_1[1], "next")]
-    far_1 = attend(1, [far_q_1], pair_1[:1])
-    back_1.append(swapped(far_1[0], "far"))
-    back_0 = later(back_0, far_1)
-    returned = [
-        in_plane(merge(own_0[0], *back_0)),
-        in_plane(merge(own_1[0], *back_1)),
+    attend = lambda group, queries, after, split=1: prefix_part(
+        queries, keys, values, group, after, split
+    )
+    half, span = slots // 2, queries.shape[1] // GROUPS
+    own = [
+        [whole[h * half : (h + 1) * half, g * span : (g + 1) * span] for h in range(2)]
+        for g in range(GROUPS)
     ]
+    near = [[swapped(x, "near") for x in block] for block in own]
+    after = [[swapped(x, "next") for x in block] for block in own]
+    far = [[swapped(a[0], "near"), swapped(n[1], "next")] for n, a in zip(near, after)]
+
+    def folded(pair, far):
+        top, low = swapped(far[0], "near"), swapped(far[1], "next")
+        return fold(pair[0], low, half), fold(pair[1], top, 0)
+
+    def back(sent):
+        return swapped(sent[0], "near"), swapped(sent[1], "next")
+
+    (own_0,) = attend(0, [own[0]], [stat])
+    pair_0 = attend(0, [near[0], after[0]], [own_0])
+    far_0 = attend(0, [far[0]], pair_0, 2)
+    far_1 = attend(1, [far[1]], far_0, 2)
+    sent_0 = folded(pair_0, far_0)
+    pair_1 = attend(1, [near[1], after[1]], [*far_1, *sent_0])
+    sent_1 = folded(pair_1, far_1)
+    (own_1,) = attend(1, [own[1]], sent_1)
+    first = in_plane(merge([own_0, *back(sent_0)], pair_1))
+    second = in_plane(merge([own_1, *back(sent_1)], [first]))
+    returned = [first, second]
     return final_part(returned, pick, mean, stat)
 
 

time: 158 us -> 153 us (0.968)
  waiting for transfers between devices: 33.7 us -> 17.5 us
  starting transfers between devices: 41 us -> 46.6 us
  local copies, waits for them, and re-layouts: 12.3 us -> 17.6 us
    ppermute x12 -> x20, waiting for transfers between devices: 17.5 us -> 0.05 us  [swapped(): return lax.ppermute(x, 'z', list(enumerate(pairs)))]
    unnamed x19 -> x31, local copies, waits for them, and re-layouts: 6.75 us -> 12.1 us
    ppermute x12 -> x20, starting transfers between devices: 16.2 us -> 20.5 us  [swapped(): return lax.ppermute(x, 'z', list(enumerate(pairs)))]
    pallas_call x8 -> x12, Pallas kernels: 57.2 us -> 56.7 us  [the longest x6 52.6 us: prefix_part(): pl.pallas_call(functools.partial(prefix_kernel, rows, many, split), grid=...]
  transfers between devices with their start and end apart: 15 -> 23, of which waited for: 6 -> 2; matrix products, arithmetic and copies ran while one was open for 1% -> 1% of each run, Pallas kernels for 43% -> 43%
where the time goes in v2:
time: 153 us; the launch traced here: 152 us
  Pallas kernels  69.5 us (45%)
  starting transfers between devices  46.6 us (30%)
  local copies, waits for them, and re-layouts  17.6 us (12%)
  waiting for transfers between devices  17.5 us (11%)
    pallas_call x6, Pallas kernels, prefix_part(): pl.pallas_call(functools.partial(prefix_kernel, rows, many, split), grid=...  52.6 us
    all_to_all x3, starting transfers between devices, in_plane(): lax.all_to_all(x, ('prefix', 'xh'), split_axis=0, concat_axis=0, tiled=True)  26.1 us
    ppermute x20, starting transfers between devices, swapped(): return lax.ppermute(x, 'z', list(enumerate(pairs)))  20.5 us
    all_to_all x3, waiting for transfers between devices, in_plane(): lax.all_to_all(x, ('prefix', 'xh'), split_axis=0, concat_axis=0, tiled=True)  17.5 us
    unnamed x31, local copies, waits for them, and re-layouts  12.1 us
    pallas_call x1, Pallas kernels, suffix_part(): pl.pallas_call(suffix_kernel, grid_spec=pltpu.PrefetchScalarGridSpec(num_...  9.94 us
    all_to_all x6, local copies, waits for them, and re-layouts, in_plane(): lax.all_to_all(x, ('prefix', 'xh'), split_axis=0, concat_axis=0, tiled=True)  5.45 us
  transfers between devices with their start and end apart: 23, of which 2 were waited for; matrix products, arithmetic and copies ran while one was open for 1% of the time, Pallas kernels for 43%

profile of v2, /device:TPU:1, one launch (start us, length us, event | category | flops | bytes accessed | tf_op | source)
XLA Modules:
  0.0 152.0 jit_solution(6072495979798217986)
XLA Ops:
  0.0 1.0 copy-done
  1.6 1.2 outgoing_queries.1
  2.8 1.5 all_to_all.22
  4.3 8.6 %all-to-all-start = ((bf16[32,2,8192]{2,1,0:T(2,128)(2,1)}), bf16[32,2,8192]{2,1,0:T(2,128)(2,1)S(1)}, u32[]{:S(2)}, u32[]{:S(2)}) async-start(bf16[32,2,8192]{2,1,0:T(2,128)(2,1)} %all_to_all.22), calls=%async_computation | async-start | bytes 2097152 | tf_op jit(solution)/shard_map/all_to_all | solution.py:326
  14.0 9.9 %suffix_attention.1 = (f32[16,64,128]{2,1,0:T(8,128)}, f32[16,1,128]{2,1,0:T(1,128)}) custom-call(s32[16]{0:T(128)} %length_ref.1, s32[16]{0:T(128)} %slot_ref.1, bf16[16,64,128]{2,1,0:T(8,128)(2,1)} %bitcast.22, bf16[16,128,1024]{2,1,0:T(8,128)(2,1)} %k_ref.1, bf16[16,128,1024]{2,1,0:T(8,128)(2,1)} %v_ref.1), custom_call_target="tpu_custom_call" | custom-call | flops 11500000256 | tf_op jit(solution)/shard_map/suffix_attention/pallas_call | solution.py:263
  23.9 6.0 %all-to-all-done = bf16[32,2,8192]{2,1,0:T(2,128)(2,1)S(1)} async-done(((bf16[32,2,8192]{2,1,0:T(2,128)(2,1)}), bf16[32,2,8192]{2,1,0:T(2,128)(2,1)S(1)}, u32[]{:S(2)}, u32[]{:S(2)}) %all-to-all-start) | async-done | bytes 1048608 | tf_op jit(solution)/shard_map/all_to_all | solution.py:326
  30.4 3.8 %collective-permute-start.3 = (bf16[32,4096]{1,0:T(8,128)(2,1)S(1)}, bf16[32,4096]{1,0:T(8,128)(2,1)S(1)}, u32[]{:S(2)}, u32[]{:S(2)}) collective-permute-start(bf16[32,4096]{1,0:T(8,128)(2,1)S(1)} %get-tuple-element.27.refs_1_), channel_id=1, source_target_pairs={{0,3},{1,2},{2,1},{3,0},{4,7},{5,6},{6,5},{7,4},{8,11},{9,10},{10,... | collective-permute-start | bytes 786440 | tf_op jit(solution)/shard_map/ppermute | solution.py:322
  34.5 1.2 collective-permute-start
  35.7 2.1 %collective-permute-start.13 = (bf16[32,4096]{1,0:T(8,128)(2,1)S(1)}, bf16[32,4096]{1,0:T(8,128)(2,1)S(1)}, u32[]{:S(2)}, u32[]{:S(2)}) collective-permute-start(bf16[32,4096]{1,0:T(8,128)(2,1)S(1)} %get-tuple-element.25.refs_1_), channel_id=1, source_target_pairs={{0,3},{1,2},{2,1},{3,0},{4,7},{5,6},{6,5},{7,4},{8,11},{9,10},{10,... | collective-permute-start | bytes 786440 | tf_op jit(solution)/shard_map/ppermute | solution.py:322
  37.8 2.2 %copy-done.8 = bf16[1,2048,1024]{2,1,0:T(8,128)(2,1)S(1)} copy-done((bf16[1,2048,1024]{2,1,0:T(8,128)(2,1)S(1)}, bf16[1,2048,1024]{2,1,0:T(8,128)(2,1)}, u32[]{:S(2)}) %copy-start.8) | copy-done | bytes 4194328
  40.0 2.2 %copy-done.11 = bf16[1,2048,1024]{2,1,0:T(8,128)(2,1)S(1)} copy-done((bf16[1,2048,1024]{2,1,0:T(8,128)(2,1)S(1)}, bf16[1,2048,1024]{2,1,0:T(8,128)(2,1)}, u32[]{:S(2)}) %copy-start.11) | copy-done | bytes 4194328
  42.2 7.1 %prefix_attention.6.refs_6_.refs_0_ = bf16[64,4224]{1,0:T(8,128)(2,1)S(1)} custom-call(bf16[32,4096]{1,0:T(8,128)(2,1)S(1)} %get-tuple-element.28.refs_0_, bf16[32,4096]{1,0:T(8,128)(2,1)S(1)} %get-tuple-element.27.refs_1_, bf16[2048,1024]{1,0:T(8,128)(2,1)S(1)} %bitcast.10, bf16[2048,1024]{1,0:T(8,128)(2,1)S(1)} %bitcast.16, f32[16,1,128]{2,1,0:T(1,128)S(1)} %copy-done.5), custom_call_target="tpu_custom_call" | custom-call | flops 4024999936 | tf_op jit(solution)/shard_map/prefix_attention/pallas_call | solution.py:125
  50.1 2.1 %collective-permute-start.5 = (bf16[32,4096]{1,0:T(8,128)(2,1)S(1)}, bf16[32,4096]{1,0:T(8,128)(2,1)S(1)}, u32[]{:S(2)}, u32[]{:S(2)}) collective-permute-start(bf16[32,4096]{1,0:T(8,128)(2,1)S(1)} %collective-permute-done.1.refs_1_), channel_id=1, source_target_pairs={{0,3},{1,2},{2,1},{3,0},{4,7},{5,6},{6,5},{7,4},{8,11},{9,10},{10,... | collective-permute-start | bytes 786440 | tf_op jit(solution)/shard_map/ppermute | solution.py:322
  52.3 12.1 %prefix_attention.7 = (bf16[64,4224]{1,0:T(8,128)(2,1)S(1)}, bf16[64,4224]{1,0:T(8,128)(2,1)S(1)}) custom-call(bf16[32,4096]{1,0:T(8,128)(2,1)S(1)} %collective-permute-done.refs_0_, bf16[32,4096]{1,0:T(8,128)(2,1)S(1)} %collective-permute-done.1.refs_1_, bf16[32,4096]{1,0:T(8,128)(2,1)S(1)} %collective-permute-done.2.refs_2_, ...), custom_call_target="tpu_custom_call" | custom-call | flops 7474999808 | tf_op jit(solution)/shard_map/prefix_attention/pallas_call | solution.py:125
  64.5 1.4 collective-permute-start.10
  66.5 7.1 %prefix_attention.8 = (bf16[32,4224]{1,0:T(8,128)(2,1)S(1)}, bf16[32,4224]{1,0:T(8,128)(2,1)S(1)}) custom-call(bf16[32,4096]{1,0:T(8,128)(2,1)S(1)} %collective-permute-done.4.refs_0_, bf16[32,4096]{1,0:T(8,128)(2,1)S(1)} %collective-permute-done.5.refs_1_, bf16[2048,1024]{1,0:T(8,128)(2,1)S(1)} %bitcast.12, bf16[2048,1024]{1,0:T(8,128)(2,1)S(1)} %bitcast.18, ...), custom_call_target="tpu_custom_call" | custom-call | flops 4024999936 | tf_op jit(solution)/shard_map/prefix_attention/pallas_call | solution.py:125
  73.6 2.1 %collective-permute-start.6 = (bf16[32,4224]{1,0:T(8,128)(2,1)S(1)}, bf16[32,4224]{1,0:T(8,128)(2,1)S(1)}, u32[]{:S(2)}, u32[]{:S(2)}) collective-permute-start(bf16[32,4224]{1,0:T(8,128)(2,1)S(1)} %get-tuple-element.18.refs_5_), channel_id=1, source_target_pairs={{0,3},{1,2},{2,1},{3,0},{4,7},{5,6},{6,5},{7,4},{8,11},{9,10},{10,... | collective-permute-start | bytes 811016 | tf_op jit(solution)/shard_map/ppermute | solution.py:322
  76.6 7.1 %prefix_attention.9 = (bf16[32,4224]{1,0:T(8,128)(2,1)S(1)}, bf16[32,4224]{1,0:T(8,128)(2,1)S(1)}) custom-call(bf16[32,4096]{1,0:T(8,128)(2,1)S(1)} %collective-permute-done.14.refs_0_, bf16[32,4096]{1,0:T(8,128)(2,1)S(1)} %collective-permute-done.15.refs_1_, bf16[2048,1024]{1,0:T(8,128)(2,1)S(1)} %bitcast.13, bf16[2048,1024]{1,0:T(8,128)(2,1)S(1)} %bitcast.19, ...), custom_call_target="tpu_custom_call" | custom-call | flops 4024999936 | tf_op jit(solution)/shard_map/prefix_attention/pallas_call | solution.py:125
  85.5 2.1 %collective-permute-start.9 = (bf16[64,4224]{1,0:T(8,128)(2,1)S(1)}, bf16[64,4224]{1,0:T(8,128)(2,1)S(1)}, u32[]{:S(2)}, u32[]{:S(2)}) collective-permute-start(bf16[64,4224]{1,0:T(8,128)(2,1)S(1)} %fold_partials.5.refs_9_), channel_id=1, source_target_pairs={{0,3},{1,2},{2,1},{3,0},{4,7},{5,6},{6,5},{7,4},{8,11},{9,10},{10,... | collective-permute-start | bytes 1622024 | tf_op jit(solution)/shard_map/ppermute | solution.py:322
  88.2 12.2 %prefix_attention.10 = (bf16[64,4224]{1,0:T(8,128)(2,1)S(1)}, bf16[64,4224]{1,0:T(8,128)(2,1)S(1)}) custom-call(bf16[32,4096]{1,0:T(8,128)(2,1)S(1)} %collective-permute-done.10.refs_0_, bf16[32,4096]{1,0:T(8,128)(2,1)S(1)} %collective-permute-done.11.refs_1_, bf16[32,4096]{1,0:T(8,128)(2,1)S(1)} %collective-permute-done.12.refs_2_, ...), custom_call_target="tpu_custom_call" | custom-call | flops 7474999808 | tf_op jit(solution)/shard_map/prefix_attention/pallas_call | solution.py:125
  103.0 1.1 merge_partials.2
  104.1 1.1 all_to_all.25
  105.1 10.1 %all-to-all-start.1 = ((bf16[32,2,4224]{2,1,0:T(2,128)(2,1)}), bf16[32,2,4224]{2,1,0:T(2,128)(2,1)}, u32[]{:S(2)}, u32[]{:S(2)}) async-start(bf16[32,2,4224]{2,1,0:T(2,128)(2,1)} %all_to_all.25), calls=%async_computation.1 | async-start | bytes 1081344 | tf_op jit(solution)/shard_map/all_to_all | solution.py:326
  116.2 2.2 %copy-done.10 = bf16[1,2048,1024]{2,1,0:T(8,128)(2,1)S(1)} copy-done((bf16[1,2048,1024]{2,1,0:T(8,128)(2,1)S(1)}, bf16[1,2048,1024]{2,1,0:T(8,128)(2,1)}, u32[]{:S(2)}) %copy-start.10) | copy-done | bytes 4194328
  118.4 2.2 %copy-done.13 = bf16[1,2048,1024]{2,1,0:T(8,128)(2,1)S(1)} copy-done((bf16[1,2048,1024]{2,1,0:T(8,128)(2,1)S(1)}, bf16[1,2048,1024]{2,1,0:T(8,128)(2,1)}, u32[]{:S(2)}) %copy-start.13) | copy-done | bytes 4194328
  120.6 7.1 %prefix_attention.11.refs_0_ = bf16[64,4224]{1,0:T(8,128)(2,1)S(1)} custom-call(bf16[32,4096]{1,0:T(8,128)(2,1)S(1)} %copy-done.4, bf16[32,4096]{1,0:T(8,128)(2,1)S(1)} %get-tuple-element.25.refs_1_, bf16[2048,1024]{1,0:T(8,128)(2,1)S(1)} %bitcast.15, bf16[2048,1024]{1,0:T(8,128)(2,1)S(1)} %bitcast.21, bf16[64,4224]{1,0:T(8,128)(2,1)S(1)} %fold_partials.6.refs_4_, ...), custom_call_target="tpu_custom_call" | custom-call | flops 4024999936 | tf_op jit(solution)/shard_map/prefix_attention/pallas_call | solution.py:125
  127.7 1.3 all_to_all.27.refs_3_.refs_0_
  129.0 1.1 merge_partials.3
  130.0 1.0 all_to_all.28
  131.1 7.4 %all-to-all-start.2 = ((bf16[32,2,4224]{2,1,0:T(2,128)(2,1)}), bf16[32,2,4224]{2,1,0:T(2,128)(2,1)S(1)}, u32[]{:S(2)}, u32[]{:S(2)}) async-start(bf16[32,2,4224]{2,1,0:T(2,128)(2,1)} %all_to_all.28), calls=%async_computation.2 | async-start | bytes 1081344 | tf_op jit(solution)/shard_map/all_to_all | solution.py:326
  138.6 11.5 %all-to-all-done.2 = bf16[32,2,4224]{2,1,0:T(2,128)(2,1)S(1)} async-done(((bf16[32,2,4224]{2,1,0:T(2,128)(2,1)}), bf16[32,2,4224]{2,1,0:T(2,128)(2,1)S(1)}, u32[]{:S(2)}, u32[]{:S(2)}) %all-to-all-start.2) | async-done | bytes 540704 | tf_op jit(solution)/shard_map/all_to_all | solution.py:326
  150.3 1.7 %last_merge.1 = bf16[16,8192]{1,0:T(8,128)(2,1)} custom-call(bf16[64,4224]{1,0:T(8,128)(2,1)S(1)} %all_to_all.27.refs_3_.refs_0_, bf16[64,4224]{1,0:T(8,128)(2,1)S(1)} %all_to_all.30.refs_1_, bf16[2,16,64]{2,1,0:T(8,128)(2,1)S(1)} %add_convert_fusion.refs_2_, f32[16,64,128]{2,1,0:T(8,128)S(1)} %copy-done.2, f32[16,1,128]{2,1,0:T(1,128)S(1)} %copy-done.5), custom_call_target="tpu_custom_call" | custom-call | tf_op jit(solution)/shard_map/last_merge/pallas_call | solution.py:312
  (75 shorter events, 11.1 us)
Async XLA Ops:
  0.0 12.9 %copy-start.7 = (s32[16]{0:T(128)S(1)}, s32[16]{0:T(128)}, u32[]{:S(2)}) copy-start(s32[16]{0:T(128)} %param.9) | copy-start | bytes 196
  1.6 11.5 %copy-start.1 = (bf16[16,8192]{1,0:T(8,128)(2,1)S(1)}, bf16[16,8192]{1,0:T(8,128)(2,1)}, u32[]{:S(2)}) copy-start(bf16[16,8192]{1,0:T(8,128)(2,1)} %q_ref.1) | copy-start | bytes 786436
  4.3 25.5 %all-to-all-start = ((bf16[32,2,8192]{2,1,0:T(2,128)(2,1)}), bf16[32,2,8192]{2,1,0:T(2,128)(2,1)S(1)}, u32[]{:S(2)}, u32[]{:S(2)}) async-start(bf16[32,2,8192]{2,1,0:T(2,128)(2,1)} %all_to_all.22), calls=%async_computation | async-start | bytes 2097152 | tf_op jit(solution)/shard_map/all_to_all | solution.py:326
  23.9 13.9 %copy-start.5 = (f32[16,1,128]{2,1,0:T(1,128)S(1)}, f32[16,1,128]{2,1,0:T(1,128)}, u32[]{:S(2)}) copy-start(f32[16,1,128]{2,1,0:T(1,128)} %get-tuple-element.15.refs_4_) | copy-start | bytes 24580
  30.4 34.1 %copy-start.3 = (bf16[32,4096]{1,0:T(8,128)(2,1)}, bf16[32,4096]{1,0:T(8,128)(2,1)S(1)}, u32[]{:S(2)}) copy-start(bf16[32,4096]{1,0:T(8,128)(2,1)S(1)} %get-tuple-element.26.refs_0_) | copy-start | bytes 786436
  30.4 18.9 %collective-permute-start.3 = (bf16[32,4096]{1,0:T(8,128)(2,1)S(1)}, bf16[32,4096]{1,0:T(8,128)(2,1)S(1)}, u32[]{:S(2)}, u32[]{:S(2)}) collective-permute-start(bf16[32,4096]{1,0:T(8,128)(2,1)S(1)} %get-tuple-element.27.refs_1_), channel_id=1, source_target_pairs={{0,3},{1,2},{2,1},{3,0},{4,7},{5,6},{6,5},{7,4},{8,11},{9,10},{10,... | collective-permute-start | bytes 786440 | tf_op jit(solution)/shard_map/ppermute | solution.py:322
  34.2 15.1 %collective-permute-start.1 = (bf16[32,4096]{1,0:T(8,128)(2,1)S(1)}, bf16[32,4096]{1,0:T(8,128)(2,1)S(1)}, u32[]{:S(2)}, u32[]{:S(2)}) collective-permute-start(bf16[32,4096]{1,0:T(8,128)(2,1)S(1)} %get-tuple-element.27.refs_1_), channel_id=1, source_target_pairs={{0,1},{1,0},{2,3},{3,2},{4,5},{5,4},{6,7},{7,6},{8,9},{9,8},{10,11... | collective-permute-start | bytes 786440 | tf_op jit(solution)/shard_map/ppermute | solution.py:322
  34.2 15.8 %collective-permute-start.2 = (bf16[32,4096]{1,0:T(8,128)(2,1)S(1)}, bf16[32,4096]{1,0:T(8,128)(2,1)S(1)}, u32[]{:S(2)}, u32[]{:S(2)}) collective-permute-start(bf16[32,4096]{1,0:T(8,128)(2,1)S(1)} %get-tuple-element.28.refs_0_), channel_id=1, source_target_pairs={{0,3},{1,2},{2,1},{3,0},{4,7},{5,6},{6,5},{7,4},{8,11},{9,10},{10,... | collective-permute-start | bytes 786440 | tf_op jit(solution)/shard_map/ppermute | solution.py:322
  34.5 17.7 %collective-permute-start = (bf16[32,4096]{1,0:T(8,128)(2,1)S(1)}, bf16[32,4096]{1,0:T(8,128)(2,1)S(1)}, u32[]{:S(2)}, u32[]{:S(2)}) collective-permute-start(bf16[32,4096]{1,0:T(8,128)(2,1)S(1)} %get-tuple-element.28.refs_0_), channel_id=1, source_target_pairs={{0,1},{1,0},{2,3},{3,2},{4,5},{5,4},{6,7},{7,6},{8,9},{9,8},{10,11... | collective-permute-start | bytes 786440 | tf_op jit(solution)/shard_map/ppermute | solution.py:322
  35.7 52.4 %collective-permute-start.13 = (bf16[32,4096]{1,0:T(8,128)(2,1)S(1)}, bf16[32,4096]{1,0:T(8,128)(2,1)S(1)}, u32[]{:S(2)}, u32[]{:S(2)}) collective-permute-start(bf16[32,4096]{1,0:T(8,128)(2,1)S(1)} %get-tuple-element.25.refs_1_), channel_id=1, source_target_pairs={{0,3},{1,2},{2,1},{3,0},{4,7},{5,6},{6,5},{7,4},{8,11},{9,10},{10,... | collective-permute-start | bytes 786440 | tf_op jit(solution)/shard_map/ppermute | solution.py:322
  37.8 2.2 %copy-start.8 = (bf16[1,2048,1024]{2,1,0:T(8,128)(2,1)S(1)}, bf16[1,2048,1024]{2,1,0:T(8,128)(2,1)}, u32[]{:S(2)}) copy-start(bf16[1,2048,1024]{2,1,0:T(8,128)(2,1)} %param.12) | copy-start | bytes 12582916
  42.2 10.1 %copy-start.9 = (bf16[1,2048,1024]{2,1,0:T(8,128)(2,1)S(1)}, bf16[1,2048,1024]{2,1,0:T(8,128)(2,1)}, u32[]{:S(2)}) copy-start(bf16[1,2048,1024]{2,1,0:T(8,128)(2,1)} %param.12) | copy-start | bytes 12582916
  49.3 15.2 %collective-permute-start.11 = (bf16[32,4096]{1,0:T(8,128)(2,1)S(1)}, bf16[32,4096]{1,0:T(8,128)(2,1)S(1)}, u32[]{:S(2)}, u32[]{:S(2)}) collective-permute-start(bf16[32,4096]{1,0:T(8,128)(2,1)S(1)} %get-tuple-element.25.refs_1_), channel_id=1, source_target_pairs={{0,1},{1,0},{2,3},{3,2},{4,5},{5,4},{6,7},{7,6},{8,9},{9,8},{10,11... | collective-permute-start | bytes 786440 | tf_op jit(solution)/shard_map/ppermute | solution.py:322
  49.4 16.5 %collective-permute-start.12 = (bf16[32,4096]{1,0:T(8,128)(2,1)S(1)}, bf16[32,4096]{1,0:T(8,128)(2,1)S(1)}, u32[]{:S(2)}, u32[]{:S(2)}) collective-permute-start(bf16[32,4096]{1,0:T(8,128)(2,1)S(1)} %get-tuple-element.26.refs_0_), channel_id=1, source_target_pairs={{0,3},{1,2},{2,1},{3,0},{4,7},{5,6},{6,5},{7,4},{8,11},{9,10},{10,... | collective-permute-start | bytes 786440 | tf_op jit(solution)/shard_map/ppermute | solution.py:322
  50.1 16.4 %collective-permute-start.5 = (bf16[32,4096]{1,0:T(8,128)(2,1)S(1)}, bf16[32,4096]{1,0:T(8,128)(2,1)S(1)}, u32[]{:S(2)}, u32[]{:S(2)}) collective-permute-start(bf16[32,4096]{1,0:T(8,128)(2,1)S(1)} %collective-permute-done.1.refs_1_), channel_id=1, source_target_pairs={{0,3},{1,2},{2,1},{3,0},{4,7},{5,6},{6,5},{7,4},{8,11},{9,10},{10,... | collective-permute-start | bytes 786440 | tf_op jit(solution)/shard_map/ppermute | solution.py:322
  52.1 14.3 %collective-permute-start.4 = (bf16[32,4096]{1,0:T(8,128)(2,1)S(1)}, bf16[32,4096]{1,0:T(8,128)(2,1)S(1)}, u32[]{:S(2)}, u32[]{:S(2)}) collective-permute-start(bf16[32,4096]{1,0:T(8,128)(2,1)S(1)} %collective-permute-done.2.refs_2_), channel_id=1, source_target_pairs={{0,1},{1,0},{2,3},{3,2},{4,5},{5,4},{6,7},{7,6},{8,9},{9,8},{10,11... | collective-permute-start | bytes 786440 | tf_op jit(solution)/shard_map/ppermute | solution.py:322
  64.5 23.7 %collective-permute-start.10 = (bf16[32,4096]{1,0:T(8,128)(2,1)S(1)}, bf16[32,4096]{1,0:T(8,128)(2,1)S(1)}, u32[]{:S(2)}, u32[]{:S(2)}) collective-permute-start(bf16[32,4096]{1,0:T(8,128)(2,1)S(1)} %get-tuple-element.26.refs_0_), channel_id=1, source_target_pairs={{0,1},{1,0},{2,3},{3,2},{4,5},{5,4},{6,7},{7,6},{8,9},{9,8},{10,11... | collective-permute-start | bytes 786440 | tf_op jit(solution)/shard_map/ppermute | solution.py:322
  65.8 9.9 %collective-permute-start.15 = (bf16[32,4096]{1,0:T(8,128)(2,1)S(1)}, bf16[32,4096]{1,0:T(8,128)(2,1)S(1)}, u32[]{:S(2)}, u32[]{:S(2)}) collective-permute-start(bf16[32,4096]{1,0:T(8,128)(2,1)S(1)} %collective-permute-done.11.refs_1_), channel_id=1, source_target_pairs={{0,3},{1,2},{2,1},{3,0},{4,7},{5,6},{6,5},{7,4},{8,11},{9,10},{10,... | collective-permute-start | bytes 786440 | tf_op jit(solution)/shard_map/ppermute | solution.py:322
  66.5 10.1 %collective-permute-start.14 = (bf16[32,4096]{1,0:T(8,128)(2,1)S(1)}, bf16[32,4096]{1,0:T(8,128)(2,1)S(1)}, u32[]{:S(2)}, u32[]{:S(2)}) collective-permute-start(bf16[32,4096]{1,0:T(8,128)(2,1)S(1)} %collective-permute-done.12.refs_2_), channel_id=1, source_target_pairs={{0,1},{1,0},{2,3},{3,2},{4,5},{5,4},{6,7},{7,6},{8,9},{9,8},{10,11... | collective-permute-start | bytes 786440 | tf_op jit(solution)/shard_map/ppermute | solution.py:322
  66.5 10.1 %copy-start.12 = (bf16[1,2048,1024]{2,1,0:T(8,128)(2,1)S(1)}, bf16[1,2048,1024]{2,1,0:T(8,128)(2,1)}, u32[]{:S(2)}) copy-start(bf16[1,2048,1024]{2,1,0:T(8,128)(2,1)} %param.13) | copy-start | bytes 12582916
  73.6 11.9 %collective-permute-start.6 = (bf16[32,4224]{1,0:T(8,128)(2,1)S(1)}, bf16[32,4224]{1,0:T(8,128)(2,1)S(1)}, u32[]{:S(2)}, u32[]{:S(2)}) collective-permute-start(bf16[32,4224]{1,0:T(8,128)(2,1)S(1)} %get-tuple-element.18.refs_5_), channel_id=1, source_target_pairs={{0,3},{1,2},{2,1},{3,0},{4,7},{5,6},{6,5},{7,4},{8,11},{9,10},{10,... | collective-permute-start | bytes 811016 | tf_op jit(solution)/shard_map/ppermute | solution.py:322
  75.7 8.6 %collective-permute-start.8 = (bf16[32,4224]{1,0:T(8,128)(2,1)S(1)}, bf16[32,4224]{1,0:T(8,128)(2,1)S(1)}, u32[]{:S(2)}, u32[]{:S(2)}) collective-permute-start(bf16[32,4224]{1,0:T(8,128)(2,1)S(1)} %get-tuple-element.19.refs_4_), channel_id=1, source_target_pairs={{0,1},{1,0},{2,3},{3,2},{4,5},{5,4},{6,7},{7,6},{8,9},{9,8},{10,11... | collective-permute-start | bytes 811016 | tf_op jit(solution)/shard_map/ppermute | solution.py:322
  83.6 16.8 %collective-permute-start.17 = (bf16[32,4224]{1,0:T(8,128)(2,1)S(1)}, bf16[32,4224]{1,0:T(8,128)(2,1)S(1)}, u32[]{:S(2)}, u32[]{:S(2)}) collective-permute-start(bf16[32,4224]{1,0:T(8,128)(2,1)S(1)} %get-tuple-element.20.refs_6_), channel_id=1, source_target_pairs={{0,1},{1,0},{2,3},{3,2},{4,5},{5,4},{6,7},{7,6},{8,9},{9,8},{10,11... | collective-permute-start | bytes 811016 | tf_op jit(solution)/shard_map/ppermute | solution.py:322
  84.3 17.3 %collective-permute-start.16 = (bf16[32,4224]{1,0:T(8,128)(2,1)S(1)}, bf16[32,4224]{1,0:T(8,128)(2,1)S(1)}, u32[]{:S(2)}, u32[]{:S(2)}) collective-permute-start(bf16[32,4224]{1,0:T(8,128)(2,1)S(1)} %get-tuple-element.21.refs_7_), channel_id=1, source_target_pairs={{0,3},{1,2},{2,1},{3,0},{4,7},{5,6},{6,5},{7,4},{8,11},{9,10},{10,... | collective-permute-start | bytes 811016 | tf_op jit(solution)/shard_map/ppermute | solution.py:322
  85.5 17.6 %collective-permute-start.9 = (bf16[64,4224]{1,0:T(8,128)(2,1)S(1)}, bf16[64,4224]{1,0:T(8,128)(2,1)S(1)}, u32[]{:S(2)}, u32[]{:S(2)}) collective-permute-start(bf16[64,4224]{1,0:T(8,128)(2,1)S(1)} %fold_partials.5.refs_9_), channel_id=1, source_target_pairs={{0,3},{1,2},{2,1},{3,0},{4,7},{5,6},{6,5},{7,4},{8,11},{9,10},{10,... | collective-permute-start | bytes 1622024 | tf_op jit(solution)/shard_map/ppermute | solution.py:322
  88.1 14.9 %collective-permute-start.7 = (bf16[64,4224]{1,0:T(8,128)(2,1)S(1)}, bf16[64,4224]{1,0:T(8,128)(2,1)S(1)}, u32[]{:S(2)}, u32[]{:S(2)}) collective-permute-start(bf16[64,4224]{1,0:T(8,128)(2,1)S(1)} %fold_partials.4.refs_8_), channel_id=1, source_target_pairs={{0,1},{1,0},{2,3},{3,2},{4,5},{5,4},{6,7},{7,6},{8,9},{9,8},{10,11... | collective-permute-start | bytes 1622024 | tf_op jit(solution)/shard_map/ppermute | solution.py:322
  100.4 14.9 %copy-start.14 = (s32[16]{0:T(128)S(1)}, s32[16]{0:T(128)}, u32[]{:S(2)}) copy-start(s32[16]{0:T(128)} %slot_ref.1) | copy-start | bytes 196
  100.9 28.0 %collective-permute-start.19 = (bf16[64,4224]{1,0:T(8,128)(2,1)S(1)}, bf16[64,4224]{1,0:T(8,128)(2,1)S(1)}, u32[]{:S(2)}, u32[]{:S(2)}) collective-permute-start(bf16[64,4224]{1,0:T(8,128)(2,1)S(1)} %fold_partials.7.refs_5_), channel_id=1, source_target_pairs={{0,3},{1,2},{2,1},{3,0},{4,7},{5,6},{6,5},{7,4},{8,11},{9,10},{10,... | collective-permute-start | bytes 1622024 | tf_op jit(solution)/shard_map/ppermute | solution.py:322
  102.1 26.9 %collective-permute-start.18 = (bf16[64,4224]{1,0:T(8,128)(2,1)S(1)}, bf16[64,4224]{1,0:T(8,128)(2,1)S(1)}, u32[]{:S(2)}, u32[]{:S(2)}) collective-permute-start(bf16[64,4224]{1,0:T(8,128)(2,1)S(1)} %fold_partials.6.refs_4_), channel_id=1, source_target_pairs={{0,1},{1,0},{2,3},{3,2},{4,5},{5,4},{6,7},{7,6},{8,9},{9,8},{10,11... | collective-permute-start | bytes 1622024 | tf_op jit(solution)/shard_map/ppermute | solution.py:322
  105.1 22.6 %all-to-all-start.1 = ((bf16[32,2,4224]{2,1,0:T(2,128)(2,1)}), bf16[32,2,4224]{2,1,0:T(2,128)(2,1)}, u32[]{:S(2)}, u32[]{:S(2)}) async-start(bf16[32,2,4224]{2,1,0:T(2,128)(2,1)} %all_to_all.25), calls=%async_computation.1 | async-start | bytes 1081344 | tf_op jit(solution)/shard_map/all_to_all | solution.py:326
  129.0 21.4 %copy-start.2 = (f32[16,64,128]{2,1,0:T(8,128)S(1)}, f32[16,64,128]{2,1,0:T(8,128)}, u32[]{:S(2)}) copy-start(f32[16,64,128]{2,1,0:T(8,128)} %get-tuple-element.24.refs_3_) | copy-start | bytes 1572868
  131.1 19.1 %all-to-all-start.2 = ((bf16[32,2,4224]{2,1,0:T(2,128)(2,1)}), bf16[32,2,4224]{2,1,0:T(2,128)(2,1)S(1)}, u32[]{:S(2)}, u32[]{:S(2)}) async-start(bf16[32,2,4224]{2,1,0:T(2,128)(2,1)} %all_to_all.28), calls=%async_computation.2 | async-start | bytes 1081344 | tf_op jit(solution)/shard_map/all_to_all | solution.py:326
  (6 other events, 9.1 us)

commit v3 on v2

--- a/solution.py
+++ b/solution.py
@@ -382,9 +382,9 @@
     pair_1 = attend(1, [near[1], after[1]], [*far_1, *sent_0])
     sent_1 = folded(pair_1, far_1)
     (own_1,) = attend(1, [own[1]], sent_1)
-    first = in_plane(merge([own_0, *back(sent_0)], pair_1))
-    second = in_plane(merge([own_1, *back(sent_1)], [first]))
-    returned = [first, second]
+    results = [merge([own_0, *back(sent_0)], [own_1]), merge([own_1, *back(sent_1)])]
+    returned = in_plane(jnp.concatenate(results, axis=1))
+    returned = [returned[:, : span + 128], returned[:, span + 128 :]]
     return final_part(returned, pick, mean, stat)
 
 

time: 153 us -> 145 us (0.948)
  starting transfers between devices: 46.6 us -> 39.2 us
  waiting for transfers between devices: 17.5 us -> 23.8 us
  local copies, waits for them, and re-layouts: 17.6 us -> 11.5 us
    all_to_all x3 -> x2, starting transfers between devices: 26.1 us -> 18.3 us  [in_plane(): lax.all_to_all(x, ('prefix', 'xh'), split_axis=0, concat_axis=0, tiled=True)]
    all_to_all x3 -> x2, waiting for transfers between devices: 17.5 us -> 23.1 us  [in_plane(): lax.all_to_all(x, ('prefix', 'xh'), split_axis=0, concat_axis=0, tiled=True)]
    unnamed x31 -> x23, local copies, waits for them, and re-layouts: 12.1 us -> 7.71 us
    all_to_all x6 -> x4, local copies, waits for them, and re-layouts: 5.45 us -> 3.63 us  [in_plane(): lax.all_to_all(x, ('prefix', 'xh'), split_axis=0, concat_axis=0, tiled=True)]
  transfers between devices with their start and end apart: 23 -> 22, of which waited for: 2 -> 4; matrix products, arithmetic and copies ran while one was open for 1% -> 1% of each run, Pallas kernels for 43% -> 45%
where the time goes in v3:
time: 145 us
  Pallas kernels  69.5 us (48%)
  starting transfers between devices  39.2 us (27%)
  waiting for transfers between devices  23.8 us (16%)
  local copies, waits for them, and re-layouts  11.5 us (8%)
    pallas_call x6, Pallas kernels, prefix_part(): pl.pallas_call(functools.partial(prefix_kernel, rows, many, split), grid=...  52.6 us
    all_to_all x2, waiting for transfers between devices, in_plane(): lax.all_to_all(x, ('prefix', 'xh'), split_axis=0, concat_axis=0, tiled=True)  23.1 us
    ppermute x20, starting transfers between devices, swapped(): return lax.ppermute(x, 'z', list(enumerate(pairs)))  20.9 us
    all_to_all x2, starting transfers between devices, in_plane(): lax.all_to_all(x, ('prefix', 'xh'), split_axis=0, concat_axis=0, tiled=True)  18.3 us
    pallas_call x1, Pallas kernels, suffix_part(): pl.pallas_call(suffix_kernel, grid_spec=pltpu.PrefetchScalarGridSpec(num_...  9.92 us
    unnamed x23, local copies, waits for them, and re-layouts  7.71 us
    all_to_all x4, local copies, waits for them, and re-layouts, in_plane(): lax.all_to_all(x, ('prefix', 'xh'), split_axis=0, concat_axis=0, tiled=True)  3.63 us
  transfers between devices with their start and end apart: 22, of which 4 were waited for; matrix products, arithmetic and copies ran while one was open for 1% of the time, Pallas kernels for 45%

profile of v3, /device:TPU:1, one launch (start us, length us, event | category | flops | bytes accessed | tf_op | source)
XLA Modules:
  0.0 144.9 jit_solution(9764566777538291328)
XLA Ops:
  0.0 0.9 copy-done
  1.6 1.2 outgoing_queries.1
  2.8 1.5 %all_to_all.16 = bf16[32,2,8192]{2,1,0:T(2,128)(2,1)} reshape(bf16[64,8192]{1,0:T(8,128)(2,1)S(1)} %outgoing_queries.1) | data formatting | bytes 2097152 | tf_op jit(solution)/shard_map/all_to_all | solution.py:326
  4.3 8.7 %all-to-all-start = ((bf16[32,2,8192]{2,1,0:T(2,128)(2,1)}), bf16[32,2,8192]{2,1,0:T(2,128)(2,1)S(1)}, u32[]{:S(2)}, u32[]{:S(2)}) async-start(bf16[32,2,8192]{2,1,0:T(2,128)(2,1)} %all_to_all.16), calls=%async_computation | async-start | bytes 2097152 | tf_op jit(solution)/shard_map/all_to_all | solution.py:326
  13.1 0.8 copy.9
  13.8 9.9 %suffix_attention.1 = (f32[16,64,128]{2,1,0:T(8,128)}, f32[16,1,128]{2,1,0:T(1,128)}) custom-call(s32[16]{0:T(128)} %length_ref.1, s32[16]{0:T(128)} %slot_ref.1, bf16[16,64,128]{2,1,0:T(8,128)(2,1)} %bitcast.22, bf16[16,128,1024]{2,1,0:T(8,128)(2,1)} %k_ref.1, bf16[16,128,1024]{2,1,0:T(8,128)(2,1)} %v_ref.1), custom_call_target="tpu_custom_call" | custom-call | flops 11500000256 | tf_op jit(solution)/shard_map/suffix_attention/pallas_call | solution.py:263
  23.7 6.3 %all-to-all-done = bf16[32,2,8192]{2,1,0:T(2,128)(2,1)S(1)} async-done(((bf16[32,2,8192]{2,1,0:T(2,128)(2,1)}), bf16[32,2,8192]{2,1,0:T(2,128)(2,1)S(1)}, u32[]{:S(2)}, u32[]{:S(2)}) %all-to-all-start) | async-done | bytes 1048608 | tf_op jit(solution)/shard_map/all_to_all | solution.py:326
  30.5 3.8 %collective-permute-start.2 = (bf16[32,4096]{1,0:T(8,128)(2,1)S(1)}, bf16[32,4096]{1,0:T(8,128)(2,1)S(1)}, u32[]{:S(2)}, u32[]{:S(2)}) collective-permute-start(bf16[32,4096]{1,0:T(8,128)(2,1)S(1)} %get-tuple-element.30.refs_0_), channel_id=1, source_target_pairs={{0,3},{1,2},{2,1},{3,0},{4,7},{5,6},{6,5},{7,4},{8,11},{9,10},{10,... | collective-permute-start | bytes 786440 | tf_op jit(solution)/shard_map/ppermute | solution.py:322
  34.3 1.5 %collective-permute-start.1 = (bf16[32,4096]{1,0:T(8,128)(2,1)S(1)}, bf16[32,4096]{1,0:T(8,128)(2,1)S(1)}, u32[]{:S(2)}, u32[]{:S(2)}) collective-permute-start(bf16[32,4096]{1,0:T(8,128)(2,1)S(1)} %get-tuple-element.27.refs_1_), channel_id=1, source_target_pairs={{0,1},{1,0},{2,3},{3,2},{4,5},{5,4},{6,7},{7,6},{8,9},{9,8},{10,11... | collective-permute-start | bytes 786440 | tf_op jit(solution)/shard_map/ppermute | solution.py:322
  35.9 2.6 %collective-permute-start.12 = (bf16[32,4096]{1,0:T(8,128)(2,1)S(1)}, bf16[32,4096]{1,0:T(8,128)(2,1)S(1)}, u32[]{:S(2)}, u32[]{:S(2)}) collective-permute-start(bf16[32,4096]{1,0:T(8,128)(2,1)S(1)} %get-tuple-element.29.refs_0_), channel_id=1, source_target_pairs={{0,3},{1,2},{2,1},{3,0},{4,7},{5,6},{6,5},{7,4},{8,11},{9,10},{10,... | collective-permute-start | bytes 786440 | tf_op jit(solution)/shard_map/ppermute | solution.py:322
  38.5 2.2 %copy-done.6 = bf16[1,2048,1024]{2,1,0:T(8,128)(2,1)S(1)} copy-done((bf16[1,2048,1024]{2,1,0:T(8,128)(2,1)S(1)}, bf16[1,2048,1024]{2,1,0:T(8,128)(2,1)}, u32[]{:S(2)}) %copy-start.6) | copy-done | bytes 4194328
  40.7 2.2 %copy-done.8 = bf16[1,2048,1024]{2,1,0:T(8,128)(2,1)S(1)} copy-done((bf16[1,2048,1024]{2,1,0:T(8,128)(2,1)S(1)}, bf16[1,2048,1024]{2,1,0:T(8,128)(2,1)}, u32[]{:S(2)}) %copy-start.8) | copy-done | bytes 4194328
  42.9 7.1 %prefix_attention.6.refs_6_.refs_0_ = bf16[64,4224]{1,0:T(8,128)(2,1)S(1)} custom-call(bf16[32,4096]{1,0:T(8,128)(2,1)S(1)} %get-tuple-element.30.refs_0_, bf16[32,4096]{1,0:T(8,128)(2,1)S(1)} %get-tuple-element.27.refs_1_, bf16[2048,1024]{1,0:T(8,128)(2,1)S(1)} %bitcast.10, bf16[2048,1024]{1,0:T(8,128)(2,1)S(1)} %bitcast.16, f32[16,1,128]{2,1,0:T(1,128)S(1)} %copy-done.3), custom_call_target="tpu_custom_call" | custom-call | flops 4024999936 | tf_op jit(solution)/shard_map/prefix_attention/pallas_call | solution.py:125
  50.1 1.4 collective-permute-start.11
  51.7 12.1 %prefix_attention.7 = (bf16[64,4224]{1,0:T(8,128)(2,1)S(1)}, bf16[64,4224]{1,0:T(8,128)(2,1)S(1)}) custom-call(bf16[32,4096]{1,0:T(8,128)(2,1)S(1)} %collective-permute-done.refs_0_, bf16[32,4096]{1,0:T(8,128)(2,1)S(1)} %collective-permute-done.1.refs_1_, bf16[32,4096]{1,0:T(8,128)(2,1)S(1)} %collective-permute-done.2.refs_2_, ...), custom_call_target="tpu_custom_call" | custom-call | flops 7474999808 | tf_op jit(solution)/shard_map/prefix_attention/pallas_call | solution.py:125
  63.9 2.7 %collective-permute-start.13 = (bf16[32,4096]{1,0:T(8,128)(2,1)S(1)}, bf16[32,4096]{1,0:T(8,128)(2,1)S(1)}, u32[]{:S(2)}, u32[]{:S(2)}) collective-permute-start(bf16[32,4096]{1,0:T(8,128)(2,1)S(1)} %get-tuple-element.28.refs_1_), channel_id=1, source_target_pairs={{0,3},{1,2},{2,1},{3,0},{4,7},{5,6},{6,5},{7,4},{8,11},{9,10},{10,... | collective-permute-start | bytes 786440 | tf_op jit(solution)/shard_map/ppermute | solution.py:322
  67.4 7.1 %prefix_attention.8 = (bf16[32,4224]{1,0:T(8,128)(2,1)S(1)}, bf16[32,4224]{1,0:T(8,128)(2,1)S(1)}) custom-call(bf16[32,4096]{1,0:T(8,128)(2,1)S(1)} %collective-permute-done.4.refs_0_, bf16[32,4096]{1,0:T(8,128)(2,1)S(1)} %collective-permute-done.5.refs_1_, bf16[2048,1024]{1,0:T(8,128)(2,1)S(1)} %bitcast.12, bf16[2048,1024]{1,0:T(8,128)(2,1)S(1)} %bitcast.18, ...), custom_call_target="tpu_custom_call" | custom-call | flops 4024999936 | tf_op jit(solution)/shard_map/prefix_attention/pallas_call | solution.py:125
  74.5 0.7 collective-permute-start.8
  75.2 2.0 %collective-permute-start.6 = (bf16[32,4224]{1,0:T(8,128)(2,1)S(1)}, bf16[32,4224]{1,0:T(8,128)(2,1)S(1)}, u32[]{:S(2)}, u32[]{:S(2)}) collective-permute-start(bf16[32,4224]{1,0:T(8,128)(2,1)S(1)} %get-tuple-element.18.refs_5_), channel_id=1, source_target_pairs={{0,3},{1,2},{2,1},{3,0},{4,7},{5,6},{6,5},{7,4},{8,11},{9,10},{10,... | collective-permute-start | bytes 811016 | tf_op jit(solution)/shard_map/ppermute | solution.py:322
  77.3 7.1 %prefix_attention.9 = (bf16[32,4224]{1,0:T(8,128)(2,1)S(1)}, bf16[32,4224]{1,0:T(8,128)(2,1)S(1)}) custom-call(bf16[32,4096]{1,0:T(8,128)(2,1)S(1)} %collective-permute-done.14.refs_0_, bf16[32,4096]{1,0:T(8,128)(2,1)S(1)} %collective-permute-done.15.refs_1_, bf16[2048,1024]{1,0:T(8,128)(2,1)S(1)} %bitcast.13, bf16[2048,1024]{1,0:T(8,128)(2,1)S(1)} %bitcast.19, ...), custom_call_target="tpu_custom_call" | custom-call | flops 4024999936 | tf_op jit(solution)/shard_map/prefix_attention/pallas_call | solution.py:125
  85.9 2.1 %collective-permute-start.9 = (bf16[64,4224]{1,0:T(8,128)(2,1)S(1)}, bf16[64,4224]{1,0:T(8,128)(2,1)S(1)}, u32[]{:S(2)}, u32[]{:S(2)}) collective-permute-start(bf16[64,4224]{1,0:T(8,128)(2,1)S(1)} %fold_partials.5.refs_9_), channel_id=1, source_target_pairs={{0,3},{1,2},{2,1},{3,0},{4,7},{5,6},{6,5},{7,4},{8,11},{9,10},{10,... | collective-permute-start | bytes 1622024 | tf_op jit(solution)/shard_map/ppermute | solution.py:322
  88.6 12.2 %prefix_attention.10 = (bf16[64,4224]{1,0:T(8,128)(2,1)S(1)}, bf16[64,4224]{1,0:T(8,128)(2,1)S(1)}) custom-call(bf16[32,4096]{1,0:T(8,128)(2,1)S(1)} %collective-permute-done.10.refs_0_, bf16[32,4096]{1,0:T(8,128)(2,1)S(1)} %collective-permute-done.11.refs_1_, bf16[32,4096]{1,0:T(8,128)(2,1)S(1)} %collective-permute-done.12.refs_2_, ...), custom_call_target="tpu_custom_call" | custom-call | flops 7474999808 | tf_op jit(solution)/shard_map/prefix_attention/pallas_call | solution.py:125
  101.3 0.8 collective-permute-start.19
  102.6 1.0 collective-permute-start.18
  103.6 7.1 %prefix_attention.11.refs_3_.refs_0_ = bf16[64,4224]{1,0:T(8,128)(2,1)S(1)} custom-call(bf16[32,4096]{1,0:T(8,128)(2,1)S(1)} %get-tuple-element.29.refs_0_, bf16[32,4096]{1,0:T(8,128)(2,1)S(1)} %get-tuple-element.28.refs_1_, bf16[2048,1024]{1,0:T(8,128)(2,1)S(1)} %bitcast.15, bf16[2048,1024]{1,0:T(8,128)(2,1)S(1)} %bitcast.21, ...), custom_call_target="tpu_custom_call" | custom-call | flops 4024999936 | tf_op jit(solution)/shard_map/prefix_attention/pallas_call | solution.py:125
  110.7 1.1 merge_partials.2
  112.4 1.1 merge_partials.3
  113.5 1.3 all_to_all.19
  114.8 9.6 %all-to-all-start.1 = ((bf16[32,2,8448]{2,1,0:T(2,128)(2,1)}), bf16[32,2,8448]{2,1,0:T(2,128)(2,1)S(1)}, u32[]{:S(2)}, u32[]{:S(2)}) async-start(bf16[32,2,8448]{2,1,0:T(2,128)(2,1)} %all_to_all.19), calls=%async_computation.1 | async-start | bytes 2162688 | tf_op jit(solution)/shard_map/all_to_all | solution.py:326
  124.9 16.8 %all-to-all-done.1 = bf16[32,2,8448]{2,1,0:T(2,128)(2,1)S(1)} async-done(((bf16[32,2,8448]{2,1,0:T(2,128)(2,1)}), bf16[32,2,8448]{2,1,0:T(2,128)(2,1)S(1)}, u32[]{:S(2)}, u32[]{:S(2)}) %all-to-all-start.1) | async-done | bytes 1081376 | tf_op jit(solution)/shard_map/all_to_all | solution.py:326
  142.2 0.9 copy-done.2
  143.2 1.7 %last_merge.1 = bf16[16,8192]{1,0:T(8,128)(2,1)} custom-call(bf16[64,4224]{1,0:T(8,128)(2,1)S(1)} %get-tuple-element.26.refs_0_, bf16[64,4224]{1,0:T(8,128)(2,1)S(1)} %get-tuple-element.25.refs_1_, bf16[2,16,64]{2,1,0:T(8,128)(2,1)S(1)} %add_convert_fusion.refs_2_, f32[16,64,128]{2,1,0:T(8,128)S(1)} %copy-done.2, f32[16,1,128]{2,1,0:T(1,128)S(1)} %copy-done.3), custom_call_target="tpu_custom_call" | custom-call | tf_op jit(solution)/shard_map/last_merge/pallas_call | solution.py:312
  (65 shorter events, 7.1 us)
Async XLA Ops:
  0.0 0.9 copy-start
  4.3 8.7 %copy-start.1 = (bf16[16,8192]{1,0:T(8,128)(2,1)S(1)}, bf16[16,8192]{1,0:T(8,128)(2,1)}, u32[]{:S(2)}) copy-start(bf16[16,8192]{1,0:T(8,128)(2,1)} %q_ref.1) | copy-start | bytes 786436
  4.3 25.7 %all-to-all-start = ((bf16[32,2,8192]{2,1,0:T(2,128)(2,1)}), bf16[32,2,8192]{2,1,0:T(2,128)(2,1)S(1)}, u32[]{:S(2)}, u32[]{:S(2)}) async-start(bf16[32,2,8192]{2,1,0:T(2,128)(2,1)} %all_to_all.16), calls=%async_computation | async-start | bytes 2097152 | tf_op jit(solution)/shard_map/all_to_all | solution.py:326
  30.4 8.1 %copy-start.3 = (f32[16,1,128]{2,1,0:T(1,128)S(1)}, f32[16,1,128]{2,1,0:T(1,128)}, u32[]{:S(2)}) copy-start(f32[16,1,128]{2,1,0:T(1,128)} %get-tuple-element.15.refs_4_) | copy-start | bytes 24580
  30.5 19.6 %collective-permute-start.2 = (bf16[32,4096]{1,0:T(8,128)(2,1)S(1)}, bf16[32,4096]{1,0:T(8,128)(2,1)S(1)}, u32[]{:S(2)}, u32[]{:S(2)}) collective-permute-start(bf16[32,4096]{1,0:T(8,128)(2,1)S(1)} %get-tuple-element.30.refs_0_), channel_id=1, source_target_pairs={{0,3},{1,2},{2,1},{3,0},{4,7},{5,6},{6,5},{7,4},{8,11},{9,10},{10,... | collective-permute-start | bytes 786440 | tf_op jit(solution)/shard_map/ppermute | solution.py:322
  34.3 17.2 %collective-permute-start = (bf16[32,4096]{1,0:T(8,128)(2,1)S(1)}, bf16[32,4096]{1,0:T(8,128)(2,1)S(1)}, u32[]{:S(2)}, u32[]{:S(2)}) collective-permute-start(bf16[32,4096]{1,0:T(8,128)(2,1)S(1)} %get-tuple-element.30.refs_0_), channel_id=1, source_target_pairs={{0,1},{1,0},{2,3},{3,2},{4,5},{5,4},{6,7},{7,6},{8,9},{9,8},{10,11... | collective-permute-start | bytes 786440 | tf_op jit(solution)/shard_map/ppermute | solution.py:322
  34.3 15.6 %collective-permute-start.1 = (bf16[32,4096]{1,0:T(8,128)(2,1)S(1)}, bf16[32,4096]{1,0:T(8,128)(2,1)S(1)}, u32[]{:S(2)}, u32[]{:S(2)}) collective-permute-start(bf16[32,4096]{1,0:T(8,128)(2,1)S(1)} %get-tuple-element.27.refs_1_), channel_id=1, source_target_pairs={{0,1},{1,0},{2,3},{3,2},{4,5},{5,4},{6,7},{7,6},{8,9},{9,8},{10,11... | collective-permute-start | bytes 786440 | tf_op jit(solution)/shard_map/ppermute | solution.py:322
  35.8 15.8 %collective-permute-start.3 = (bf16[32,4096]{1,0:T(8,128)(2,1)S(1)}, bf16[32,4096]{1,0:T(8,128)(2,1)S(1)}, u32[]{:S(2)}, u32[]{:S(2)}) collective-permute-start(bf16[32,4096]{1,0:T(8,128)(2,1)S(1)} %get-tuple-element.27.refs_1_), channel_id=1, source_target_pairs={{0,3},{1,2},{2,1},{3,0},{4,7},{5,6},{6,5},{7,4},{8,11},{9,10},{10,... | collective-permute-start | bytes 786440 | tf_op jit(solution)/shard_map/ppermute | solution.py:322
  35.9 28.0 %collective-permute-start.12 = (bf16[32,4096]{1,0:T(8,128)(2,1)S(1)}, bf16[32,4096]{1,0:T(8,128)(2,1)S(1)}, u32[]{:S(2)}, u32[]{:S(2)}) collective-permute-start(bf16[32,4096]{1,0:T(8,128)(2,1)S(1)} %get-tuple-element.29.refs_0_), channel_id=1, source_target_pairs={{0,3},{1,2},{2,1},{3,0},{4,7},{5,6},{6,5},{7,4},{8,11},{9,10},{10,... | collective-permute-start | bytes 786440 | tf_op jit(solution)/shard_map/ppermute | solution.py:322
  38.5 2.2 %copy-start.6 = (bf16[1,2048,1024]{2,1,0:T(8,128)(2,1)S(1)}, bf16[1,2048,1024]{2,1,0:T(8,128)(2,1)}, u32[]{:S(2)}) copy-start(bf16[1,2048,1024]{2,1,0:T(8,128)(2,1)} %param.12) | copy-start | bytes 12582916
  40.7 2.2 %copy-start.8 = (bf16[1,2048,1024]{2,1,0:T(8,128)(2,1)S(1)}, bf16[1,2048,1024]{2,1,0:T(8,128)(2,1)}, u32[]{:S(2)}) copy-start(bf16[1,2048,1024]{2,1,0:T(8,128)(2,1)} %param.13) | copy-start | bytes 12582916
  42.9 8.8 %copy-start.7 = (bf16[1,2048,1024]{2,1,0:T(8,128)(2,1)S(1)}, bf16[1,2048,1024]{2,1,0:T(8,128)(2,1)}, u32[]{:S(2)}) copy-start(bf16[1,2048,1024]{2,1,0:T(8,128)(2,1)} %param.12) | copy-start | bytes 12582916
  50.0 38.5 %collective-permute-start.10 = (bf16[32,4096]{1,0:T(8,128)(2,1)S(1)}, bf16[32,4096]{1,0:T(8,128)(2,1)S(1)}, u32[]{:S(2)}, u32[]{:S(2)}) collective-permute-start(bf16[32,4096]{1,0:T(8,128)(2,1)S(1)} %get-tuple-element.29.refs_0_), channel_id=1, source_target_pairs={{0,1},{1,0},{2,3},{3,2},{4,5},{5,4},{6,7},{7,6},{8,9},{9,8},{10,11... | collective-permute-start | bytes 786440 | tf_op jit(solution)/shard_map/ppermute | solution.py:322
  50.1 16.5 %collective-permute-start.11 = (bf16[32,4096]{1,0:T(8,128)(2,1)S(1)}, bf16[32,4096]{1,0:T(8,128)(2,1)S(1)}, u32[]{:S(2)}, u32[]{:S(2)}) collective-permute-start(bf16[32,4096]{1,0:T(8,128)(2,1)S(1)} %get-tuple-element.28.refs_1_), channel_id=1, source_target_pairs={{0,1},{1,0},{2,3},{3,2},{4,5},{5,4},{6,7},{7,6},{8,9},{9,8},{10,11... | collective-permute-start | bytes 786440 | tf_op jit(solution)/shard_map/ppermute | solution.py:322
  51.5 15.3 %collective-permute-start.4 = (bf16[32,4096]{1,0:T(8,128)(2,1)S(1)}, bf16[32,4096]{1,0:T(8,128)(2,1)S(1)}, u32[]{:S(2)}, u32[]{:S(2)}) collective-permute-start(bf16[32,4096]{1,0:T(8,128)(2,1)S(1)} %collective-permute-done.2.refs_2_), channel_id=1, source_target_pairs={{0,1},{1,0},{2,3},{3,2},{4,5},{5,4},{6,7},{7,6},{8,9},{9,8},{10,11... | collective-permute-start | bytes 786440 | tf_op jit(solution)/shard_map/ppermute | solution.py:322
  51.6 15.8 %collective-permute-start.5 = (bf16[32,4096]{1,0:T(8,128)(2,1)S(1)}, bf16[32,4096]{1,0:T(8,128)(2,1)S(1)}, u32[]{:S(2)}, u32[]{:S(2)}) collective-permute-start(bf16[32,4096]{1,0:T(8,128)(2,1)S(1)} %collective-permute-done.1.refs_1_), channel_id=1, source_target_pairs={{0,3},{1,2},{2,1},{3,0},{4,7},{5,6},{6,5},{7,4},{8,11},{9,10},{10,... | collective-permute-start | bytes 786440 | tf_op jit(solution)/shard_map/ppermute | solution.py:322
  63.9 24.7 %collective-permute-start.13 = (bf16[32,4096]{1,0:T(8,128)(2,1)S(1)}, bf16[32,4096]{1,0:T(8,128)(2,1)S(1)}, u32[]{:S(2)}, u32[]{:S(2)}) collective-permute-start(bf16[32,4096]{1,0:T(8,128)(2,1)S(1)} %get-tuple-element.28.refs_1_), channel_id=1, source_target_pairs={{0,3},{1,2},{2,1},{3,0},{4,7},{5,6},{6,5},{7,4},{8,11},{9,10},{10,... | collective-permute-start | bytes 786440 | tf_op jit(solution)/shard_map/ppermute | solution.py:322
  66.5 8.7 %collective-permute-start.14 = (bf16[32,4096]{1,0:T(8,128)(2,1)S(1)}, bf16[32,4096]{1,0:T(8,128)(2,1)S(1)}, u32[]{:S(2)}, u32[]{:S(2)}) collective-permute-start(bf16[32,4096]{1,0:T(8,128)(2,1)S(1)} %collective-permute-done.12.refs_2_), channel_id=1, source_target_pairs={{0,1},{1,0},{2,3},{3,2},{4,5},{5,4},{6,7},{7,6},{8,9},{9,8},{10,11... | collective-permute-start | bytes 786440 | tf_op jit(solution)/shard_map/ppermute | solution.py:322
  66.9 10.4 %collective-permute-start.15 = (bf16[32,4096]{1,0:T(8,128)(2,1)S(1)}, bf16[32,4096]{1,0:T(8,128)(2,1)S(1)}, u32[]{:S(2)}, u32[]{:S(2)}) collective-permute-start(bf16[32,4096]{1,0:T(8,128)(2,1)S(1)} %collective-permute-done.11.refs_1_), channel_id=1, source_target_pairs={{0,3},{1,2},{2,1},{3,0},{4,7},{5,6},{6,5},{7,4},{8,11},{9,10},{10,... | collective-permute-start | bytes 786440 | tf_op jit(solution)/shard_map/ppermute | solution.py:322
  67.4 9.8 %copy-start.9 = (bf16[1,2048,1024]{2,1,0:T(8,128)(2,1)S(1)}, bf16[1,2048,1024]{2,1,0:T(8,128)(2,1)}, u32[]{:S(2)}) copy-start(bf16[1,2048,1024]{2,1,0:T(8,128)(2,1)} %param.13) | copy-start | bytes 12582916
  74.5 10.2 %collective-permute-start.8 = (bf16[32,4224]{1,0:T(8,128)(2,1)S(1)}, bf16[32,4224]{1,0:T(8,128)(2,1)S(1)}, u32[]{:S(2)}, u32[]{:S(2)}) collective-permute-start(bf16[32,4224]{1,0:T(8,128)(2,1)S(1)} %get-tuple-element.19.refs_4_), channel_id=1, source_target_pairs={{0,1},{1,0},{2,3},{3,2},{4,5},{5,4},{6,7},{7,6},{8,9},{9,8},{10,11... | collective-permute-start | bytes 811016 | tf_op jit(solution)/shard_map/ppermute | solution.py:322
  75.2 10.7 %collective-permute-start.6 = (bf16[32,4224]{1,0:T(8,128)(2,1)S(1)}, bf16[32,4224]{1,0:T(8,128)(2,1)S(1)}, u32[]{:S(2)}, u32[]{:S(2)}) collective-permute-start(bf16[32,4224]{1,0:T(8,128)(2,1)S(1)} %get-tuple-element.18.refs_5_), channel_id=1, source_target_pairs={{0,3},{1,2},{2,1},{3,0},{4,7},{5,6},{6,5},{7,4},{8,11},{9,10},{10,... | collective-permute-start | bytes 811016 | tf_op jit(solution)/shard_map/ppermute | solution.py:322
  84.3 16.4 %collective-permute-start.17 = (bf16[32,4224]{1,0:T(8,128)(2,1)S(1)}, bf16[32,4224]{1,0:T(8,128)(2,1)S(1)}, u32[]{:S(2)}, u32[]{:S(2)}) collective-permute-start(bf16[32,4224]{1,0:T(8,128)(2,1)S(1)} %get-tuple-element.20.refs_6_), channel_id=1, source_target_pairs={{0,1},{1,0},{2,3},{3,2},{4,5},{5,4},{6,7},{7,6},{8,9},{9,8},{10,11... | collective-permute-start | bytes 811016 | tf_op jit(solution)/shard_map/ppermute | solution.py:322
  84.7 17.4 %collective-permute-start.16 = (bf16[32,4224]{1,0:T(8,128)(2,1)S(1)}, bf16[32,4224]{1,0:T(8,128)(2,1)S(1)}, u32[]{:S(2)}, u32[]{:S(2)}) collective-permute-start(bf16[32,4224]{1,0:T(8,128)(2,1)S(1)} %get-tuple-element.21.refs_7_), channel_id=1, source_target_pairs={{0,3},{1,2},{2,1},{3,0},{4,7},{5,6},{6,5},{7,4},{8,11},{9,10},{10,... | collective-permute-start | bytes 811016 | tf_op jit(solution)/shard_map/ppermute | solution.py:322
  85.9 24.8 %collective-permute-start.9 = (bf16[64,4224]{1,0:T(8,128)(2,1)S(1)}, bf16[64,4224]{1,0:T(8,128)(2,1)S(1)}, u32[]{:S(2)}, u32[]{:S(2)}) collective-permute-start(bf16[64,4224]{1,0:T(8,128)(2,1)S(1)} %fold_partials.5.refs_9_), channel_id=1, source_target_pairs={{0,3},{1,2},{2,1},{3,0},{4,7},{5,6},{6,5},{7,4},{8,11},{9,10},{10,... | collective-permute-start | bytes 1622024 | tf_op jit(solution)/shard_map/ppermute | solution.py:322
  88.5 22.2 %collective-permute-start.7 = (bf16[64,4224]{1,0:T(8,128)(2,1)S(1)}, bf16[64,4224]{1,0:T(8,128)(2,1)S(1)}, u32[]{:S(2)}, u32[]{:S(2)}) collective-permute-start(bf16[64,4224]{1,0:T(8,128)(2,1)S(1)} %fold_partials.4.refs_8_), channel_id=1, source_target_pairs={{0,1},{1,0},{2,3},{3,2},{4,5},{5,4},{6,7},{7,6},{8,9},{9,8},{10,11... | collective-permute-start | bytes 1622024 | tf_op jit(solution)/shard_map/ppermute | solution.py:322
  101.3 11.1 %collective-permute-start.19 = (bf16[64,4224]{1,0:T(8,128)(2,1)S(1)}, bf16[64,4224]{1,0:T(8,128)(2,1)S(1)}, u32[]{:S(2)}, u32[]{:S(2)}) collective-permute-start(bf16[64,4224]{1,0:T(8,128)(2,1)S(1)} %fold_partials.7.refs_5_), channel_id=1, source_target_pairs={{0,3},{1,2},{2,1},{3,0},{4,7},{5,6},{6,5},{7,4},{8,11},{9,10},{10,... | collective-permute-start | bytes 1622024 | tf_op jit(solution)/shard_map/ppermute | solution.py:322
  102.6 9.7 %collective-permute-start.18 = (bf16[64,4224]{1,0:T(8,128)(2,1)S(1)}, bf16[64,4224]{1,0:T(8,128)(2,1)S(1)}, u32[]{:S(2)}, u32[]{:S(2)}) collective-permute-start(bf16[64,4224]{1,0:T(8,128)(2,1)S(1)} %fold_partials.6.refs_4_), channel_id=1, source_target_pairs={{0,1},{1,0},{2,3},{3,2},{4,5},{5,4},{6,7},{7,6},{8,9},{9,8},{10,11... | collective-permute-start | bytes 1622024 | tf_op jit(solution)/shard_map/ppermute | solution.py:322
  114.8 9.6 %copy-start.5 = (s32[16]{0:T(128)S(1)}, s32[16]{0:T(128)}, u32[]{:S(2)}) copy-start(s32[16]{0:T(128)} %param.9) | copy-start | bytes 196
  114.8 9.8 %copy-start.10 = (s32[16]{0:T(128)S(1)}, s32[16]{0:T(128)}, u32[]{:S(2)}) copy-start(s32[16]{0:T(128)} %slot_ref.1) | copy-start | bytes 196
  114.8 26.9 %all-to-all-start.1 = ((bf16[32,2,8448]{2,1,0:T(2,128)(2,1)}), bf16[32,2,8448]{2,1,0:T(2,128)(2,1)S(1)}, u32[]{:S(2)}, u32[]{:S(2)}) async-start(bf16[32,2,8448]{2,1,0:T(2,128)(2,1)} %all_to_all.19), calls=%async_computation.1 | async-start | bytes 2162688 | tf_op jit(solution)/shard_map/all_to_all | solution.py:326
  142.1 1.0 copy-start.2
  (1 other events, 0.7 us)
